TPU v7x, 512 devices: a whole 4x4x16 slice. The times are simulated.
512 devices in a mesh: row: 32 (over y, x, z_hi), col: 16 (over z_lo, core).
Axes of the slice: x: 4, y: 4, z: 16 (z_hi: 2, z_lo: 8; z = z_hi * 8 + z_lo), core: 2. Of those that a mesh axis runs over, the one named last changes fastest.
Arguments:
- grads: bfloat16 [4096, 8192], P(('row', 'col')), as said below
Outputs:
- gram: float32 [4096, 4096], P('row', 'col')
Inputs may be any that keep to these rules, and one draw needn't show every extreme that they name: `grads`: each row is a real-valued projected gradient.
All inputs are finite; a program needn't handle non-finite values.
Results may differ from a plain program's by a relative error of at most 0.0003.
Values may be sent and summed in bfloat16 or wider, within the bound.
No kernel may reach another device: no remote copies, remote signals or barrier semaphores. Data moves between devices by JAX's collectives and lax.ppermute only.
A program may use at most 64 MiB of HBM per device.

v0:
```python
import jax
import jax.numpy as jnp
from jax import lax
from jax.sharding import PartitionSpec as P


def from_root(value, axis, source):
    kept = jnp.where(lax.axis_index(axis) == source, value, 0).astype(value.dtype)
    return lax.psum(kept, axis)


def inverse_norms(block):
    wide = block.astype(jnp.float32)
    return lax.rsqrt(jnp.sum(wide * wide, axis=1) + 1e-06)


def cross(left, right):
    return lax.dot_general(
        left, right, (((1,), (1,)), ((), ())), preferred_element_type=jnp.float32
    )


def body(grads):
    block = lax.all_gather(grads, "col", axis=0, tiled=True)
    left_inverse = inverse_norms(block)
    row_count = lax.axis_size("row")
    col_count = lax.axis_size("col")
    factor = row_count // col_count
    column_index = lax.axis_index("col")
    received = []
    for offset in range(factor):
        received.append(from_root(block, "row", column_index * factor + offset))
    columns = jnp.concatenate(received, axis=0)
    products = cross(block, columns)
    right_inverse = inverse_norms(columns)
    return left_inverse[:, None] * products * right_inverse[None, :]


def solution(mesh):
    in_specs = (P(("row", "col"), None),)
    out_specs = P("row", "col")
    return jax.shard_map(body, mesh=mesh, in_specs=in_specs, out_specs=out_specs, check_vma=False)
```

profile of v0, /device:TPU:48, one launch (start us, length us, event | category | flops | bytes accessed | tf_op | source)
XLA Modules:
  0.0 1005.2 jit_solution(11854702563906713860)
XLA Ops:
  6.5 0.0 all-gather.2.cloned.1.call-start
  6.5 0.7 all-gather.2.cloned.1.call-update
  7.3 0.0 all-reduce.3.cloned.1.call-start
  7.3 98.4 %all-gather.2.cloned.1.call-done = bf16[128,8192]{1,0:T(8,128)(2,1)} async-done(((bf16[8,8192]{1,0:T(8,128)(2,1)}), bf16[128,8192]{1,0:T(8,128)(2,1)}) %all-gather.2.cloned.1.call-update) | async-done | bytes 2097168 | tf_op jit(solution)/shard_map/all_gather | solution.py:24
  105.7 3.9 broadcast_select_fusion
  109.6 0.0 copy-start
  109.6 0.0 all-reduce.3.cloned.1.call-update
  109.6 1.6 copy-done
  111.2 0.5 multiply_reduce_fusion.1
  111.7 881.3 %all-reduce.3.cloned.1.call-done = (bf16[128,8192]{1,0:T(8,128)(2,1)}, bf16[128,8192]{1,0:T(8,128)(2,1)}) async-done(((bf16[128,8192]{1,0:T(8,128)(2,1)}, bf16[128,8192]{1,0:T(8,128)(2,1)}), (bf16[128,8192]{1,0:T(8,128)(2,1)}, bf16[128,8192]{1,0:T(8,128)(2,1)})) %all-reduce.3.cloned.1.call-update) | async-done | bytes 4194320 | tf_op jit(solution)/shard_map/psum | solution.py:9
  993.0 0.0 copy-start.1
  993.0 1.9 constant_dynamic-update-slice_fusion.1
  994.9 0.3 copy-done.1
  995.3 0.1 constant_dynamic-update-slice_fusion
  995.4 0.9 multiply_reduce_fusion
  996.3 1.3 fusion.1
  997.6 0.8 copy.2
  (2 shorter events, 0.0 us)
Async XLA Ops:
  6.5 99.2 %all-gather.2.cloned.1.call-start = ((), (), s32[]{:S(2)}) async-start(), calls=%async_computation | async-start | bytes 2228224 | tf_op jit(solution)/shard_map/all_gather | solution.py:24
  7.3 985.8 %all-reduce.3.cloned.1.call-start = ((), (), s32[]{:S(2)}) async-start(), calls=%async_computation.1 | async-start | bytes 8388608 | tf_op jit(solution)/shard_map/psum | solution.py:9
  109.6 1.6 copy-start
  993.0 2.2 copy-start.1
Sparse Core Ops, SparseCore 0:
  9.4 96.2 all-gather.1
  109.8 883.2 all-reduce.2
where the time goes:
time: 1010 us
  waiting for transfers between devices  980 us (97%)
  between operations  13.4 us (1%)
    psum x1, waiting for transfers between devices, from_root(): return lax.psum(kept, axis)  881 us
    all_gather x1, waiting for transfers between devices, body(): block = lax.all_gather(grads, 'col', axis=0, tiled=True)  98.4 us
  transfers between devices with their start and end apart: 2, of which 2 were waited for; matrix products, arithmetic and copies ran while one was open for 0% of the time, Pallas kernels for 0%

commit v1 on v0

v1 whole, which is shorter than its diff:
```python
import jax
import jax.numpy as jnp
from jax import lax
from jax.sharding import Mesh, PartitionSpec as P

AXES = ("y", "x", "zh", "zl", "core")
SIZES = (4, 4, 2, 8, 2)
Z = ("zh", "zl")


def inverse_norms(block):
    wide = block.astype(jnp.float32)
    return lax.rsqrt(jnp.sum(wide * wide, axis=1) + 1e-06)


def cross(left, right):
    return lax.dot_general(
        left, right, (((1,), (1,)), ((), ())), preferred_element_type=jnp.float32
    )


def linear(y, x, z, core):
    return ((y * 4 + x) * 16 + z) * 2 + core


def spread(flip):
    pairs = []
    for y in range(4):
        for x in range(4):
            for z in range(16):
                for core in range(2):
                    zl, to = 2 * y + x // 2, x % 2
                    target = linear((y + z // 4) % 4, (x + z % 4) % 4, (core ^ flip) * 8 + zl, to)
                    pairs.append((linear(y, x, z, core), target))
    return pairs


def plane_groups():
    groups = []
    for z in range(16):
        for core in range(2):
            zl = z % 8
            y, x = zl // 2, 2 * (zl % 2) + core
            groups.append([linear((y + s // 4) % 4, (x + s % 4) % 4, z, core) for s in range(16)])
    return groups


def body(grads):
    depth = grads.shape[1]
    zh, zl = lax.axis_index("zh"), lax.axis_index("zl")
    first = lax.ppermute(grads, AXES, spread(0))
    second = lax.ppermute(grads, AXES, spread(1))
    mine = jnp.where(zh == 0, jnp.concatenate([first, second]), jnp.concatenate([second, first]))
    columns = lax.all_gather(mine, AXES, axis_index_groups=plane_groups(), axis=0, tiled=True)

    rows = grads[None]
    for step in (4, 2, 1):
        other = lax.ppermute(rows, Z, [(z, z ^ step) for z in range(16)])
        rows = jnp.stack([rows, other], axis=1 if step != 4 else 0).reshape(-1, *grads.shape)
    rows = rows.reshape(8, 8, depth)
    other = lax.ppermute(rows, "core", [(0, 1), (1, 0)])
    both = jnp.stack([rows, other]).reshape(128, depth)
    left = inverse_norms(both)
    right = inverse_norms(columns)
    gram = left[:, None] * cross(both, columns) * right[None, :]
    gram = gram.reshape(2, 2, 2, 2, 8, 256)
    core = lax.axis_index("core")
    gram = jnp.where(core == 1, gram[::-1], gram)
    gram = jnp.where((zl >> 2) & 1 == 1, gram[:, ::-1], gram)
    gram = jnp.where((zl >> 1) & 1 == 1, gram[:, :, ::-1], gram)
    gram = jnp.where(zl & 1 == 1, gram[:, :, :, ::-1], gram)
    return gram.transpose(1, 2, 3, 0, 4, 5).reshape(128, 256)


def solution(mesh):
    fine = Mesh(mesh.devices.reshape(SIZES), AXES)
    return jax.shard_map(
        body, mesh=fine, in_specs=(P(AXES, None),), out_specs=P(("y", "x", "zh"), ("zl", "core")), check_vma=False
    )
```

time: 1010 us -> 151 us (0.15)
  the two profiles are of different devices: /device:TPU:48 before, /device:TPU:2 now
where the time goes in v1:
time: 151 us; the launch traced here: 150 us
  waiting for transfers between devices  93.8 us (62%)
  starting transfers between devices  32.2 us (21%)
  between operations  13.5 us (9%)
  other arithmetic  7.99 us (5%)
  matrix products  1.53 us (1%)
    all_gather x1, waiting for transfers between devices, body(): lax.all_gather(mine, AXES, axis_index_groups=plane_groups(), axis=0, tile...  42.5 us
    ppermute x3, waiting for transfers between devices, body(): other = lax.ppermute(rows, Z, [(z, z ^ step) for z in range(16)])  35 us
    ppermute x1, starting transfers between devices, body(): second = lax.ppermute(grads, AXES, spread(1))  18.1 us
    ppermute x1, waiting for transfers between devices, body(): second = lax.ppermute(grads, AXES, spread(1))  13.6 us
    ppermute x3, starting transfers between devices, body(): other = lax.ppermute(rows, Z, [(z, z ^ step) for z in range(16)])  10.3 us
    reduce_sum x2, other arithmetic, inverse_norms(): return lax.rsqrt(jnp.sum(wide * wide, axis=1) + 1e-06)  3.76 us
  transfers between devices with their start and end apart: 7, of which 6 were waited for; matrix products, arithmetic and copies ran while one was open for 3% of the time, Pallas kernels for 0%

profile of v1, /device:TPU:2, one launch (start us, length us, event | category | flops | bytes accessed | tf_op | source)
XLA Modules:
  0.0 150.4 jit_solution(14681316371964480863)
XLA Ops:
  6.5 1.9 %collective-permute-start.4 = (bf16[8,8192]{1,0:T(8,128)(2,1)}, bf16[8,8192]{1,0:T(8,128)(2,1)S(1)}, u32[]{:S(2)}, u32[]{:S(2)}) collective-permute-start(bf16[8,8192]{1,0:T(8,128)(2,1)} %param.1), channel_id=1, source_target_pairs={{0,0},{1,16},{2,32},{3,48},{4,64},{5,80},{6,96},{7,112},{8,128},{9... | collective-permute-start | bytes 393224 | tf_op jit(solution)/shard_map/ppermute | solution.py:51
  8.5 18.1 %collective-permute-start.5 = (bf16[8,8192]{1,0:T(8,128)(2,1)}, bf16[8,8192]{1,0:T(8,128)(2,1)S(1)}, u32[]{:S(2)}, u32[]{:S(2)}) collective-permute-start(bf16[8,8192]{1,0:T(8,128)(2,1)} %param.1), channel_id=1, source_target_pairs={{0,16},{1,0},{2,48},{3,32},{4,80},{5,64},{6,112},{7,96},{8,144},{9... | collective-permute-start | bytes 393224 | tf_op jit(solution)/shard_map/ppermute | solution.py:52
  26.5 13.6 %collective-permute-done.5 = bf16[8,8192]{1,0:T(8,128)(2,1)S(1)} collective-permute-done((bf16[8,8192]{1,0:T(8,128)(2,1)}, bf16[8,8192]{1,0:T(8,128)(2,1)S(1)}, u32[]{:S(2)}, u32[]{:S(2)}) %collective-permute-start.5) | collective-permute-done | bytes 131104 | tf_op jit(solution)/shard_map/ppermute | solution.py:52
  40.2 0.7 maximum_select_fusion
  40.9 2.8 %collective-permute-start = (bf16[1,8,8192]{2,1,0:T(8,128)(2,1)}, bf16[1,8,8192]{2,1,0:T(8,128)(2,1)S(1)}, u32[]{:S(2)}, u32[]{:S(2)}) collective-permute-start(bf16[1,8,8192]{2,1,0:T(8,128)(2,1)} %bitcast.29), channel_id=1, source_target_pairs={{0,8},{2,10},{4,12},{6,14},{8,0},{10,2},{12,4},{14,6},{16,24},{18,... | collective-permute-start | bytes 393224 | tf_op jit(solution)/shard_map/ppermute | solution.py:58
  43.7 12.9 %collective-permute-done = bf16[1,8,8192]{2,1,0:T(8,128)(2,1)S(1)} collective-permute-done((bf16[1,8,8192]{2,1,0:T(8,128)(2,1)}, bf16[1,8,8192]{2,1,0:T(8,128)(2,1)S(1)}, u32[]{:S(2)}, u32[]{:S(2)}) %collective-permute-start) | collective-permute-done | bytes 131104 | tf_op jit(solution)/shard_map/ppermute | solution.py:58
  56.6 0.9 maximum_bitcast_fusion
  57.6 5.6 %collective-permute-start.1 = (bf16[2,8,8192]{2,1,0:T(8,128)(2,1)S(1)}, bf16[2,8,8192]{2,1,0:T(8,128)(2,1)S(1)}, u32[]{:S(2)}, u32[]{:S(2)}) collective-permute-start(bf16[2,8,8192]{2,1,0:T(8,128)(2,1)S(1)} %maximum_bitcast_fusion), channel_id=1, source_target_pairs={{0,4},{2,6},{4,0},{6,2},{8,12},{10,14},{12,8},{14,10},{16,20},{18,... | collective-permute-start | bytes 786440 | tf_op jit(solution)/shard_map/ppermute | solution.py:58
  63.2 8.3 %collective-permute-done.1 = bf16[2,8,8192]{2,1,0:T(8,128)(2,1)S(1)} collective-permute-done((bf16[2,8,8192]{2,1,0:T(8,128)(2,1)S(1)}, bf16[2,8,8192]{2,1,0:T(8,128)(2,1)S(1)}, u32[]{:S(2)}, u32[]{:S(2)}) %collective-permute-start.1) | collective-permute-done | bytes 262176 | tf_op jit(solution)/shard_map/ppermute | solution.py:58
  71.5 1.0 pad_maximum_fusion.2
  72.4 1.9 %collective-permute-start.2 = (bf16[4,8,8192]{2,1,0:T(8,128)(2,1)S(1)}, bf16[4,8,8192]{2,1,0:T(8,128)(2,1)S(1)}, u32[]{:S(2)}, u32[]{:S(2)}) collective-permute-start(bf16[4,8,8192]{2,1,0:T(8,128)(2,1)S(1)} %bitcast.25), channel_id=1, source_target_pairs={{0,2},{2,0},{4,6},{6,4},{8,10},{10,8},{12,14},{14,12},{16,18},{18,... | collective-permute-start | bytes 1572872 | tf_op jit(solution)/shard_map/ppermute | solution.py:58
  74.3 13.8 %collective-permute-done.2 = bf16[4,8,8192]{2,1,0:T(8,128)(2,1)S(1)} collective-permute-done((bf16[4,8,8192]{2,1,0:T(8,128)(2,1)S(1)}, bf16[4,8,8192]{2,1,0:T(8,128)(2,1)S(1)}, u32[]{:S(2)}, u32[]{:S(2)}) %collective-permute-start.2) | collective-permute-done | bytes 524320 | tf_op jit(solution)/shard_map/ppermute | solution.py:58
  88.2 0.1 pad_maximum_fusion.1
  88.3 1.9 %collective-permute-start.3 = (bf16[8,8,8192]{2,1,0:T(8,128)(2,1)S(1)}, bf16[8,8,8192]{2,1,0:T(8,128)(2,1)S(1)}, u32[]{:S(2)}, u32[]{:S(2)}) collective-permute-start(bf16[8,8,8192]{2,1,0:T(8,128)(2,1)S(1)} %bitcast.19), channel_id=1, source_target_pairs={{0,1},{1,0},{2,3},{3,2},{4,5},{5,4},{6,7},{7,6},{8,9},{9,8},{10,11... | collective-permute-start | bytes 3145736 | tf_op jit(solution)/shard_map/ppermute | solution.py:61
  90.2 2.6 %collective-permute-done.3 = bf16[8,8,8192]{2,1,0:T(8,128)(2,1)S(1)} collective-permute-done((bf16[8,8,8192]{2,1,0:T(8,128)(2,1)S(1)}, bf16[8,8,8192]{2,1,0:T(8,128)(2,1)S(1)}, u32[]{:S(2)}, u32[]{:S(2)}) %collective-permute-start.3) | collective-permute-done | bytes 1048608 | tf_op jit(solution)/shard_map/ppermute | solution.py:61
  92.8 0.5 multiply_reduce_fusion.1
  93.3 0.5 copy-done.1
  93.8 0.1 rsqrt.18
  93.9 1.4 pad_maximum_fusion
  95.3 42.5 %all-gather.2.cloned.1.call-done = bf16[256,8192]{1,0:T(8,128)(2,1)} async-done(((bf16[16,8192]{1,0:T(8,128)(2,1)}), bf16[256,8192]{1,0:T(8,128)(2,1)}) %all-gather.2.cloned.1.call-update) | async-done | bytes 4194320 | tf_op jit(solution)/shard_map/all_gather | solution.py:54
  137.8 3.3 %multiply_reduce_fusion = f32[256]{0:T(256)S(1)} fusion(bf16[256,8192]{1,0:T(8,128)(2,1)} %all-gather.2.cloned.1.call-done), kind=kLoop, calls=%fused_computation | loop fusion | flops 6291200 | bytes 4195328 | tf_op jit(solution)/shard_map/reduce_sum | solution.py:13
  141.1 0.2 copy-done
  141.2 1.5 %fusion = f32[128,256]{1,0:T(8,128)S(1)} fusion(bf16[128,8192]{1,0:T(8,128)(2,1)S(1)} %bitcast.22, bf16[256,8192]{1,0:T(8,128)(2,1)S(1)} %copy-done, f32[256]{0:T(256)S(1)} %add_rsqrt_fusion.1, f32[128]{0:T(128)S(1)} %rsqrt.18), kind=kOutput, calls=%fused_computation.4 | convolution fusion | flops 536936448 | bytes 6424064 | tf_op jit(solution)/shard_map/dot_general | solution.py:17
  142.9 0.7 copy.3
  (11 shorter events, 0.1 us)
Async XLA Ops:
  6.5 131.3 %all-gather.2.cloned.1.call-start = ((), (), s32[]{:S(2)}) async-start(), calls=%async_computation | async-start | bytes 4456448 | tf_op jit(solution)/shard_map/all_gather | solution.py:54
  6.5 20.0 %collective-permute-start.4 = (bf16[8,8192]{1,0:T(8,128)(2,1)}, bf16[8,8192]{1,0:T(8,128)(2,1)S(1)}, u32[]{:S(2)}, u32[]{:S(2)}) collective-permute-start(bf16[8,8192]{1,0:T(8,128)(2,1)} %param.1), channel_id=1, source_target_pairs={{0,0},{1,16},{2,32},{3,48},{4,64},{5,80},{6,96},{7,112},{8,128},{9... | collective-permute-start | bytes 393224 | tf_op jit(solution)/shard_map/ppermute | solution.py:51
  8.5 31.7 %collective-permute-start.5 = (bf16[8,8192]{1,0:T(8,128)(2,1)}, bf16[8,8192]{1,0:T(8,128)(2,1)S(1)}, u32[]{:S(2)}, u32[]{:S(2)}) collective-permute-start(bf16[8,8192]{1,0:T(8,128)(2,1)} %param.1), channel_id=1, source_target_pairs={{0,16},{1,0},{2,48},{3,32},{4,80},{5,64},{6,112},{7,96},{8,144},{9... | collective-permute-start | bytes 393224 | tf_op jit(solution)/shard_map/ppermute | solution.py:52
  40.9 15.7 %collective-permute-start = (bf16[1,8,8192]{2,1,0:T(8,128)(2,1)}, bf16[1,8,8192]{2,1,0:T(8,128)(2,1)S(1)}, u32[]{:S(2)}, u32[]{:S(2)}) collective-permute-start(bf16[1,8,8192]{2,1,0:T(8,128)(2,1)} %bitcast.29), channel_id=1, source_target_pairs={{0,8},{2,10},{4,12},{6,14},{8,0},{10,2},{12,4},{14,6},{16,24},{18,... | collective-permute-start | bytes 393224 | tf_op jit(solution)/shard_map/ppermute | solution.py:58
  57.6 13.9 %collective-permute-start.1 = (bf16[2,8,8192]{2,1,0:T(8,128)(2,1)S(1)}, bf16[2,8,8192]{2,1,0:T(8,128)(2,1)S(1)}, u32[]{:S(2)}, u32[]{:S(2)}) collective-permute-start(bf16[2,8,8192]{2,1,0:T(8,128)(2,1)S(1)} %maximum_bitcast_fusion), channel_id=1, source_target_pairs={{0,4},{2,6},{4,0},{6,2},{8,12},{10,14},{12,8},{14,10},{16,20},{18,... | collective-permute-start | bytes 786440 | tf_op jit(solution)/shard_map/ppermute | solution.py:58
  72.4 15.7 %collective-permute-start.2 = (bf16[4,8,8192]{2,1,0:T(8,128)(2,1)S(1)}, bf16[4,8,8192]{2,1,0:T(8,128)(2,1)S(1)}, u32[]{:S(2)}, u32[]{:S(2)}) collective-permute-start(bf16[4,8,8192]{2,1,0:T(8,128)(2,1)S(1)} %bitcast.25), channel_id=1, source_target_pairs={{0,2},{2,0},{4,6},{6,4},{8,10},{10,8},{12,14},{14,12},{16,18},{18,... | collective-permute-start | bytes 1572872 | tf_op jit(solution)/shard_map/ppermute | solution.py:58
  88.3 4.6 %collective-permute-start.3 = (bf16[8,8,8192]{2,1,0:T(8,128)(2,1)S(1)}, bf16[8,8,8192]{2,1,0:T(8,128)(2,1)S(1)}, u32[]{:S(2)}, u32[]{:S(2)}) collective-permute-start(bf16[8,8,8192]{2,1,0:T(8,128)(2,1)S(1)} %bitcast.19), channel_id=1, source_target_pairs={{0,1},{1,0},{2,3},{3,2},{4,5},{5,4},{6,7},{7,6},{8,9},{9,8},{10,11... | collective-permute-start | bytes 3145736 | tf_op jit(solution)/shard_map/ppermute | solution.py:61
  92.8 1.0 copy-start.1
  137.8 3.4 %copy-start = (bf16[256,8192]{1,0:T(8,128)(2,1)S(1)}, bf16[256,8192]{1,0:T(8,128)(2,1)}, u32[]{:S(2)}) copy-start(bf16[256,8192]{1,0:T(8,128)(2,1)} %all-gather.2.cloned.1.call-done) | copy-start | bytes 12582916
Sparse Core Ops, SparseCore 0:
  41.1 96.6 all-gather.1

commit v2 on v0

v2 whole, which is shorter than its diff:
```python
import jax
import jax.numpy as jnp
from jax import lax
from jax.sharding import Mesh, PartitionSpec as P

AXES = ("y", "x", "zh", "zl", "core")
SIZES = (4, 4, 2, 8, 2)
Z = ("zh", "zl")
YZ = ("y", "zh", "zl", "core")


def squares(block):
    wide = block.astype(jnp.float32)
    return jnp.sum(wide * wide, axis=-1)


def cross(left, right):
    return lax.dot_general(
        left, right, (((1,), (1,)), ((), ())), preferred_element_type=jnp.float32
    )


def spread(half, away):
    pairs = []
    for y in range(4):
        for z in range(16):
            for core in range(2):
                m, zh = z % 2 ^ half, z // 8 ^ away
                target_y = y ^ (z // 2 % 4)
                pairs.append((((y * 16 + z) * 2) + core, ((target_y * 16 + zh * 8 + 2 * y + m) * 2) + core))
    return pairs


def swap(flag, array, axis):
    return jnp.where(flag == 1, jnp.flip(array, axis), array)


def body(grads):
    count, depth = grads.shape
    part = depth // 4
    zh, zl, core = (lax.axis_index(a) for a in ("zh", "zl", "core"))

    held = lax.all_to_all(grads.reshape(count, 4, part).transpose(1, 0, 2), "x", 0, 0, tiled=True)

    odd = zl % 2 == 1
    near = jnp.where(odd, held[2:], held[:2])
    far = jnp.where(odd, held[:2], held[2:])
    sent = [lax.ppermute(near if half == 0 else far, YZ, spread(half, away)) for half in (0, 1) for away in (0, 1)]
    mine = jnp.stack(sent)
    columns = lax.all_to_all(jnp.broadcast_to(mine[None], (4, *mine.shape)), "y", 0, 0, tiled=True)
    columns = columns.reshape(16, 2, count, part)
    own = jnp.where(core == 0, columns[:, 0], columns[:, 1])
    give = jnp.where(core == 0, columns[:, 1], columns[:, 0])
    columns = jnp.stack([own, lax.ppermute(give, "core", [(0, 1), (1, 0)])])
    columns = columns.reshape(32 * count, part)

    rows = held[:, None]
    for step in (4, 2, 1):
        other = lax.ppermute(rows, Z, [(z, z ^ step) for z in range(16)])
        rows = jnp.stack([rows, other], axis=2).reshape(4, -1, count, part)
    other = lax.ppermute(rows, "core", [(0, 1), (1, 0)])
    rows = jnp.stack([rows, other], axis=1).reshape(4, 16 * count, part)

    products = cross(rows.reshape(-1, part), columns).reshape(4, 16 * count, 32 * count)
    extra = jnp.zeros((4, 8, 32 * count), jnp.float32)
    extra = extra.at[:, 0, : 16 * count].set(squares(rows))
    extra = extra.at[:, 1].set(squares(columns)[None])
    message = jnp.concatenate([products, extra], axis=1)
    total = jnp.sum(lax.all_to_all(message, "x", 0, 0, tiled=True).reshape(4, -1, 32 * count), axis=0)
    left = lax.rsqrt(total[16 * count, : 16 * count] + 1e-06)
    right = lax.rsqrt(total[16 * count + 1] + 1e-06)
    gram = left[:, None] * total[: 16 * count] * right[None, :]

    gram = gram.reshape(2, 2, 2, 2, count, 32 * count)
    gram = swap(core, gram, 0)
    for axis, bit in ((1, 2), (2, 1), (3, 0)):
        gram = swap(zl >> bit & 1, gram, axis)
    gram = gram.transpose(1, 2, 3, 0, 4, 5).reshape(16 * count, 32 * count).T
    gram = gram.reshape(2, 2, 2, 2, 2, count, 16 * count)
    for axis, flag in ((0, core), (1, zl >> 2 & 1), (2, zl >> 1 & 1), (3, zl & 1), (4, zh)):
        gram = swap(flag, gram, axis)
    gram = gram.transpose(4, 1, 2, 3, 0, 5, 6).reshape(32 * count, 16 * count)
    return gram.T


def solution(mesh):
    fine = Mesh(mesh.devices.reshape(SIZES), AXES)
    return jax.shard_map(
        body, mesh=fine, in_specs=(P(AXES, None),), out_specs=P(("y", "x", "zh"), ("zl", "core")), check_vma=False
    )
```

time: 1010 us -> 113 us (0.11)
  the two profiles are of different devices: /device:TPU:48 before, /device:TPU:1 now
where the time goes in v2:
time: 113 us; the launch traced here: 112 us
  starting transfers between devices  65.9 us (58%)
  waiting for transfers between devices  33.7 us (30%)
  local copies, waits for them, and re-layouts  4.93 us (4%)
  other arithmetic  4.74 us (4%)
  matrix products  2.33 us (2%)
    ppermute x3, starting transfers between devices, body(): other = lax.ppermute(rows, Z, [(z, z ^ step) for z in range(16)])  18.1 us
    all_to_all x1, starting transfers between devices, body(): lax.all_to_all(jnp.broadcast_to(mine[None], (4, *mine.shape)), 'y', 0, 0,...  17.4 us
    ppermute x4, starting transfers between devices, body(): lax.ppermute(near if half == 0 else far, YZ, spread(half, away))  17 us
    all_to_all x1, waiting for transfers between devices, body(): lax.all_to_all(jnp.broadcast_to(mine[None], (4, *mine.shape)), 'y', 0, 0,...  10.3 us
    all_to_all x1, waiting for transfers between devices, body(): lax.all_to_all(message, 'x', 0, 0, tiled=True).reshape(4, -1, 32 * count)  9.78 us
    all_to_all x1, starting transfers between devices, body(): lax.all_to_all(grads.reshape(count, 4, part).transpose(1, 0, 2), 'x', 0,...  4.84 us
    all_to_all x1, waiting for transfers between devices, body(): lax.all_to_all(grads.reshape(count, 4, part).transpose(1, 0, 2), 'x', 0,...  4.83 us
    ppermute x3, waiting for transfers between devices, body(): other = lax.ppermute(rows, Z, [(z, z ^ step) for z in range(16)])  4.55 us
  transfers between devices with their start and end apart: 12, of which 7 were waited for; matrix products, arithmetic and copies ran while one was open for 3% of the time, Pallas kernels for 0%

profile of v2, /device:TPU:1, one launch (start us, length us, event | category | flops | bytes accessed | tf_op | source)
XLA Modules:
  0.0 112.0 jit_solution(6268956557479191279)
XLA Ops:
  0.0 4.8 %all-to-all-start = ((bf16[4,8,2048]{2,1,0:T(8,128)(2,1)}), bf16[4,8,2048]{2,1,0:T(8,128)(2,1)S(1)}, u32[]{:S(2)}, u32[]{:S(2)}) async-start(bf16[4,8,2048]{2,1,0:T(8,128)(2,1)} %bitcast.87), calls=%async_computation | async-start | bytes 262144 | tf_op jit(solution)/shard_map/all_to_all | solution.py:43
  4.8 4.8 %all-to-all-done = bf16[4,8,2048]{2,1,0:T(8,128)(2,1)S(1)} async-done(((bf16[4,8,2048]{2,1,0:T(8,128)(2,1)}), bf16[4,8,2048]{2,1,0:T(8,128)(2,1)S(1)}, u32[]{:S(2)}, u32[]{:S(2)}) %all-to-all-start) | async-done | bytes 131104 | tf_op jit(solution)/shard_map/all_to_all | solution.py:43
  9.7 8.8 %collective-permute-start = (bf16[4,1,8,2048]{3,2,0,1:T(8,128)(2,1)S(1)}, bf16[4,1,8,2048]{3,2,0,1:T(8,128)(2,1)S(1)}, u32[]{:S(2)}, u32[]{:S(2)}) collective-permute-start(bf16[4,1,8,2048]{3,2,0,1:T(8,128)(2,1)S(1)} %bitcast.78), channel_id=1, source_target_pairs={{0,8},{2,10},{4,12},{6,14},{8,0},{10,2},{12,4},{14,6},{16,24},{18,... | collective-permute-start | bytes 393224 | tf_op jit(solution)/shard_map/ppermute | solution.py:59
  18.5 10.2 %collective-permute-start.7 = (bf16[2,8,2048]{2,1,0:T(8,128)(2,1)S(1)}, bf16[2,8,2048]{2,1,0:T(8,128)(2,1)S(1)}, u32[]{:S(2)}, u32[]{:S(2)}) collective-permute-start(bf16[2,8,2048]{2,1,0:T(8,128)(2,1)S(1)} %get-tuple-element.32), channel_id=1, source_target_pairs={{0,18},{1,19},{2,16},{3,17},{4,146},{5,147},{6,144},{7,145},{8,274... | collective-permute-start | bytes 196616 | tf_op jit(solution)/shard_map/ppermute | solution.py:48
  28.7 2.6 %collective-permute-start.6 = (bf16[2,8,2048]{2,1,0:T(8,128)(2,1)S(1)}, bf16[2,8,2048]{2,1,0:T(8,128)(2,1)S(1)}, u32[]{:S(2)}, u32[]{:S(2)}) collective-permute-start(bf16[2,8,2048]{2,1,0:T(8,128)(2,1)S(1)} %get-tuple-element.32), channel_id=1, source_target_pairs={{0,2},{1,3},{2,0},{3,1},{4,130},{5,131},{6,128},{7,129},{8,258},{9... | collective-permute-start | bytes 196616 | tf_op jit(solution)/shard_map/ppermute | solution.py:48
  31.4 3.5 %collective-permute-start.5 = (bf16[2,8,2048]{2,1,0:T(8,128)(2,1)S(1)}, bf16[2,8,2048]{2,1,0:T(8,128)(2,1)S(1)}, u32[]{:S(2)}, u32[]{:S(2)}) collective-permute-start(bf16[2,8,2048]{2,1,0:T(8,128)(2,1)S(1)} %get-tuple-element.31), channel_id=1, source_target_pairs={{0,16},{1,17},{2,18},{3,19},{4,144},{5,145},{6,146},{7,147},{8,272... | collective-permute-start | bytes 196616 | tf_op jit(solution)/shard_map/ppermute | solution.py:48
  35.6 7.3 %collective-permute-start.1 = (bf16[4,2,8,2048]{3,2,1,0:T(8,128)(2,1)S(1)}, bf16[4,2,8,2048]{3,2,1,0:T(8,128)(2,1)S(1)}, u32[]{:S(2)}, u32[]{:S(2)}) collective-permute-start(bf16[4,2,8,2048]{3,2,1,0:T(8,128)(2,1)S(1)} %get-tuple-element.30), channel_id=1, source_target_pairs={{0,4},{2,6},{4,0},{6,2},{8,12},{10,14},{12,8},{14,10},{16,20},{18,... | collective-permute-start | bytes 786440 | tf_op jit(solution)/shard_map/ppermute | solution.py:59
  43.0 2.4 %collective-permute-done.5 = bf16[2,8,2048]{2,1,0:T(8,128)(2,1)S(1)} collective-permute-done((bf16[2,8,2048]{2,1,0:T(8,128)(2,1)S(1)}, bf16[2,8,2048]{2,1,0:T(8,128)(2,1)S(1)}, u32[]{:S(2)}, u32[]{:S(2)}) %collective-permute-start.5) | collective-permute-done | bytes 65568 | tf_op jit(solution)/shard_map/ppermute | solution.py:48
  45.4 1.1 broadcast_in_dim.7
  46.5 17.4 %all-to-all-start.1 = ((bf16[4,4,2,8,2048]{4,3,1,2,0:T(8,128)(2,1)}), bf16[4,4,2,8,2048]{4,3,1,2,0:T(8,128)(2,1)S(1)}, u32[]{:S(2)}, u32[]{:S(2)}) async-start(bf16[4,4,2,8,2048]{4,3,1,2,0:T(8,128)(2,1)} %broadcast_in_dim.7), calls=%async_computation.1 | async-start | bytes 2097152 | tf_op jit(solution)/shard_map/all_to_all | solution.py:50
  63.9 2.0 %collective-permute-done.1 = bf16[4,2,8,2048]{3,2,1,0:T(8,128)(2,1)S(1)} collective-permute-done((bf16[4,2,8,2048]{3,2,1,0:T(8,128)(2,1)S(1)}, bf16[4,2,8,2048]{3,2,1,0:T(8,128)(2,1)S(1)}, u32[]{:S(2)}, u32[]{:S(2)}) %collective-permute-start.1) | collective-permute-done | bytes 262176 | tf_op jit(solution)/shard_map/ppermute | solution.py:59
  66.0 1.9 %collective-permute-start.2 = (bf16[4,4,8,2048]{3,2,1,0:T(8,128)(2,1)S(1)}, bf16[4,4,8,2048]{3,2,1,0:T(8,128)(2,1)S(1)}, u32[]{:S(2)}, u32[]{:S(2)}) collective-permute-start(bf16[4,4,8,2048]{3,2,1,0:T(8,128)(2,1)S(1)} %bitcast.74), channel_id=1, source_target_pairs={{0,2},{2,0},{4,6},{6,4},{8,10},{10,8},{12,14},{14,12},{16,18},{18,... | collective-permute-start | bytes 1572872 | tf_op jit(solution)/shard_map/ppermute | solution.py:59
  67.9 10.3 %all-to-all-done.1 = bf16[4,4,2,8,2048]{4,3,1,2,0:T(8,128)(2,1)S(1)} async-done(((bf16[4,4,2,8,2048]{4,3,1,2,0:T(8,128)(2,1)}), bf16[4,4,2,8,2048]{4,3,1,2,0:T(8,128)(2,1)S(1)}, u32[]{:S(2)}, u32[]{:S(2)}) %all-to-all-start.1) | async-done | bytes 1048608 | tf_op jit(solution)/shard_map/all_to_all | solution.py:50
  78.3 2.5 %collective-permute-done.2 = bf16[4,4,8,2048]{3,2,1,0:T(8,128)(2,1)S(1)} collective-permute-done((bf16[4,4,8,2048]{3,2,1,0:T(8,128)(2,1)S(1)}, bf16[4,4,8,2048]{3,2,1,0:T(8,128)(2,1)S(1)}, u32[]{:S(2)}, u32[]{:S(2)}) %collective-permute-start.2) | collective-permute-done | bytes 524320 | tf_op jit(solution)/shard_map/ppermute | solution.py:59
  81.1 3.2 %collective-permute-start.3 = (bf16[4,8,8,2048]{3,2,1,0:T(8,128)(2,1)S(1)}, bf16[4,8,8,2048]{3,2,1,0:T(8,128)(2,1)S(1)}, u32[]{:S(2)}, u32[]{:S(2)}) collective-permute-start(bf16[4,8,8,2048]{3,2,1,0:T(8,128)(2,1)S(1)} %bitcast.68), channel_id=1, source_target_pairs={{0,1},{1,0},{2,3},{3,2},{4,5},{5,4},{6,7},{7,6},{8,9},{9,8},{10,11... | collective-permute-start | bytes 3145736 | tf_op jit(solution)/shard_map/ppermute | solution.py:61
  84.4 1.9 %collective-permute-start.8 = (bf16[16,8,2048]{2,1,0:T(8,128)(2,1)S(1)}, bf16[16,8,2048]{2,1,0:T(8,128)(2,1)S(1)}, u32[]{:S(2)}, u32[]{:S(2)}) collective-permute-start(bf16[16,8,2048]{2,1,0:T(8,128)(2,1)S(1)} %fusion), channel_id=1, source_target_pairs={{0,1},{1,0},{2,3},{3,2},{4,5},{5,4},{6,7},{7,6},{8,9},{9,8},{10,11... | collective-permute-start | bytes 1572872 | tf_op jit(solution)/shard_map/ppermute | solution.py:54
  86.4 1.8 %collective-permute-done.8 = bf16[16,8,2048]{2,1,0:T(8,128)(2,1)S(1)} collective-permute-done((bf16[16,8,2048]{2,1,0:T(8,128)(2,1)S(1)}, bf16[16,8,2048]{2,1,0:T(8,128)(2,1)S(1)}, u32[]{:S(2)}, u32[]{:S(2)}) %collective-permute-start.8) | collective-permute-done | bytes 524320 | tf_op jit(solution)/shard_map/ppermute | solution.py:54
  88.6 1.1 pad_maximum_fusion.2
  89.7 1.0 copy-done
  91.1 1.4 %pad_maximum_fusion = bf16[4,2,8,8,2048]{4,3,2,0,1:T(8,128)(2,1)S(1)} fusion(bf16[4,1,8,8,2048]{4,3,2,0,1:T(8,128)(2,1)} %bitcast.72, bf16[4,1,8,8,2048]{4,3,2,0,1:T(8,128)(2,1)S(1)} %bitcast.70), kind=kLoop, calls=%fused_computation.1 | loop fusion | flops 1048576 | bytes 4194304 | tf_op jit(solution)/shard_map/stack | solution.py:62
  92.6 1.5 %copy.34 = bf16[4,2,8,8,2048]{4,3,2,1,0:T(8,128)(2,1)} copy(bf16[4,2,8,8,2048]{4,3,2,0,1:T(8,128)(2,1)S(1)} %pad_maximum_fusion) | data formatting | bytes 4194304 | tf_op jit(solution)/shard_map/stack | solution.py:62
  94.2 2.3 %fusion.10 = f32[4,128,256]{2,1,0:T(8,128)S(1)} fusion(bf16[4,128,2048]{2,1,0:T(8,128)(2,1)} %bitcast.73, bf16[256,2048,1]{1,0,2:T(8,128)(2,1)S(1)} %bitcast.80), kind=kOutput, calls=%fused_computation.35 | convolution fusion | flops 536870912 | bytes 3670016 | tf_op jit(solution)/shard_map/dot_general | solution.py:18
  97.4 3.5 %all-to-all-start.2 = ((f32[4,136,256]{2,1,0:T(8,128)}), f32[4,136,256]{2,1,0:T(8,128)S(1)}, u32[]{:S(2)}, u32[]{:S(2)}) async-start(f32[4,136,256]{2,1,0:T(8,128)} %pad_maximum_fusion.3), calls=%async_computation.2 | async-start | bytes 1114112 | tf_op jit(solution)/shard_map/all_to_all | solution.py:69
  100.9 9.8 %all-to-all-done.2 = f32[4,136,256]{2,1,0:T(8,128)S(1)} async-done(((f32[4,136,256]{2,1,0:T(8,128)}), f32[4,136,256]{2,1,0:T(8,128)S(1)}, u32[]{:S(2)}, u32[]{:S(2)}) %all-to-all-start.2) | async-done | bytes 557088 | tf_op jit(solution)/shard_map/all_to_all | solution.py:69
  (45 shorter events, 4.3 us)
Async XLA Ops:
  0.0 9.7 %all-to-all-start = ((bf16[4,8,2048]{2,1,0:T(8,128)(2,1)}), bf16[4,8,2048]{2,1,0:T(8,128)(2,1)S(1)}, u32[]{:S(2)}, u32[]{:S(2)}) async-start(bf16[4,8,2048]{2,1,0:T(8,128)(2,1)} %bitcast.87), calls=%async_computation | async-start | bytes 262144 | tf_op jit(solution)/shard_map/all_to_all | solution.py:43
  9.7 25.9 %collective-permute-start = (bf16[4,1,8,2048]{3,2,0,1:T(8,128)(2,1)S(1)}, bf16[4,1,8,2048]{3,2,0,1:T(8,128)(2,1)S(1)}, u32[]{:S(2)}, u32[]{:S(2)}) collective-permute-start(bf16[4,1,8,2048]{3,2,0,1:T(8,128)(2,1)S(1)} %bitcast.78), channel_id=1, source_target_pairs={{0,8},{2,10},{4,12},{6,14},{8,0},{10,2},{12,4},{14,6},{16,24},{18,... | collective-permute-start | bytes 393224 | tf_op jit(solution)/shard_map/ppermute | solution.py:59
  18.5 24.5 %collective-permute-start.7 = (bf16[2,8,2048]{2,1,0:T(8,128)(2,1)S(1)}, bf16[2,8,2048]{2,1,0:T(8,128)(2,1)S(1)}, u32[]{:S(2)}, u32[]{:S(2)}) collective-permute-start(bf16[2,8,2048]{2,1,0:T(8,128)(2,1)S(1)} %get-tuple-element.32), channel_id=1, source_target_pairs={{0,18},{1,19},{2,16},{3,17},{4,146},{5,147},{6,144},{7,145},{8,274... | collective-permute-start | bytes 196616 | tf_op jit(solution)/shard_map/ppermute | solution.py:48
  28.7 14.3 %collective-permute-start.6 = (bf16[2,8,2048]{2,1,0:T(8,128)(2,1)S(1)}, bf16[2,8,2048]{2,1,0:T(8,128)(2,1)S(1)}, u32[]{:S(2)}, u32[]{:S(2)}) collective-permute-start(bf16[2,8,2048]{2,1,0:T(8,128)(2,1)S(1)} %get-tuple-element.32), channel_id=1, source_target_pairs={{0,2},{1,3},{2,0},{3,1},{4,130},{5,131},{6,128},{7,129},{8,258},{9... | collective-permute-start | bytes 196616 | tf_op jit(solution)/shard_map/ppermute | solution.py:48
  31.4 14.0 %collective-permute-start.5 = (bf16[2,8,2048]{2,1,0:T(8,128)(2,1)S(1)}, bf16[2,8,2048]{2,1,0:T(8,128)(2,1)S(1)}, u32[]{:S(2)}, u32[]{:S(2)}) collective-permute-start(bf16[2,8,2048]{2,1,0:T(8,128)(2,1)S(1)} %get-tuple-element.31), channel_id=1, source_target_pairs={{0,16},{1,17},{2,18},{3,19},{4,144},{5,145},{6,146},{7,147},{8,272... | collective-permute-start | bytes 196616 | tf_op jit(solution)/shard_map/ppermute | solution.py:48
  34.9 10.4 %collective-permute-start.4 = (bf16[2,8,2048]{2,1,0:T(8,128)(2,1)S(1)}, bf16[2,8,2048]{2,1,0:T(8,128)(2,1)S(1)}, u32[]{:S(2)}, u32[]{:S(2)}) collective-permute-start(bf16[2,8,2048]{2,1,0:T(8,128)(2,1)S(1)} %get-tuple-element.31), channel_id=1, source_target_pairs={{0,0},{1,1},{2,2},{3,3},{4,128},{5,129},{6,130},{7,131},{8,256},{9... | collective-permute-start | bytes 196616 | tf_op jit(solution)/shard_map/ppermute | solution.py:48
  35.6 30.3 %collective-permute-start.1 = (bf16[4,2,8,2048]{3,2,1,0:T(8,128)(2,1)S(1)}, bf16[4,2,8,2048]{3,2,1,0:T(8,128)(2,1)S(1)}, u32[]{:S(2)}, u32[]{:S(2)}) collective-permute-start(bf16[4,2,8,2048]{3,2,1,0:T(8,128)(2,1)S(1)} %get-tuple-element.30), channel_id=1, source_target_pairs={{0,4},{2,6},{4,0},{6,2},{8,12},{10,14},{12,8},{14,10},{16,20},{18,... | collective-permute-start | bytes 786440 | tf_op jit(solution)/shard_map/ppermute | solution.py:59
  46.5 31.7 %all-to-all-start.1 = ((bf16[4,4,2,8,2048]{4,3,1,2,0:T(8,128)(2,1)}), bf16[4,4,2,8,2048]{4,3,1,2,0:T(8,128)(2,1)S(1)}, u32[]{:S(2)}, u32[]{:S(2)}) async-start(bf16[4,4,2,8,2048]{4,3,1,2,0:T(8,128)(2,1)} %broadcast_in_dim.7), calls=%async_computation.1 | async-start | bytes 2097152 | tf_op jit(solution)/shard_map/all_to_all | solution.py:50
  66.0 14.9 %collective-permute-start.2 = (bf16[4,4,8,2048]{3,2,1,0:T(8,128)(2,1)S(1)}, bf16[4,4,8,2048]{3,2,1,0:T(8,128)(2,1)S(1)}, u32[]{:S(2)}, u32[]{:S(2)}) collective-permute-start(bf16[4,4,8,2048]{3,2,1,0:T(8,128)(2,1)S(1)} %bitcast.74), channel_id=1, source_target_pairs={{0,2},{2,0},{4,6},{6,4},{8,10},{10,8},{12,14},{14,12},{16,18},{18,... | collective-permute-start | bytes 1572872 | tf_op jit(solution)/shard_map/ppermute | solution.py:59
  81.1 8.6 %collective-permute-start.3 = (bf16[4,8,8,2048]{3,2,1,0:T(8,128)(2,1)S(1)}, bf16[4,8,8,2048]{3,2,1,0:T(8,128)(2,1)S(1)}, u32[]{:S(2)}, u32[]{:S(2)}) collective-permute-start(bf16[4,8,8,2048]{3,2,1,0:T(8,128)(2,1)S(1)} %bitcast.68), channel_id=1, source_target_pairs={{0,1},{1,0},{2,3},{3,2},{4,5},{5,4},{6,7},{7,6},{8,9},{9,8},{10,11... | collective-permute-start | bytes 3145736 | tf_op jit(solution)/shard_map/ppermute | solution.py:61
  84.4 3.8 %collective-permute-start.8 = (bf16[16,8,2048]{2,1,0:T(8,128)(2,1)S(1)}, bf16[16,8,2048]{2,1,0:T(8,128)(2,1)S(1)}, u32[]{:S(2)}, u32[]{:S(2)}) collective-permute-start(bf16[16,8,2048]{2,1,0:T(8,128)(2,1)S(1)} %fusion), channel_id=1, source_target_pairs={{0,1},{1,0},{2,3},{3,2},{4,5},{5,4},{6,7},{7,6},{8,9},{9,8},{10,11... | collective-permute-start | bytes 1572872 | tf_op jit(solution)/shard_map/ppermute | solution.py:54
  89.6 1.0 copy-start
  92.6 1.6 %copy-start.1 = (bf16[2,16,8,2048]{3,2,1,0:T(8,128)(2,1)S(1)}, bf16[2,16,8,2048]{3,2,1,0:T(8,128)(2,1)}, u32[]{:S(2)}) copy-start(bf16[2,16,8,2048]{3,2,1,0:T(8,128)(2,1)} %pad_maximum_fusion.2) | copy-start | bytes 3145732
  97.4 13.3 %all-to-all-start.2 = ((f32[4,136,256]{2,1,0:T(8,128)}), f32[4,136,256]{2,1,0:T(8,128)S(1)}, u32[]{:S(2)}, u32[]{:S(2)}) async-start(f32[4,136,256]{2,1,0:T(8,128)} %pad_maximum_fusion.3), calls=%async_computation.2 | async-start | bytes 1114112 | tf_op jit(solution)/shard_map/all_to_all | solution.py:69

commit v3 on v0

v3 whole, which is shorter than its diff:
```python
import jax
import jax.numpy as jnp
from jax import lax
from jax.sharding import Mesh, PartitionSpec as P

AXES = ("y", "x", "zh", "za", "zb", "core")
SIZES = (4, 4, 2, 4, 2, 2)
SUM = ("y", "zb")


def squares(block):
    wide = block.astype(jnp.float32)
    return jnp.sum(wide * wide, axis=-1)


def cross(left, right):
    return lax.dot_general(
        left, right, (((1,), (1,)), ((), ())), preferred_element_type=jnp.float32
    )


def swap(flag, array, axis):
    return jnp.where(flag == 1, jnp.flip(array, axis), array)


def to_all(array, axes, size):
    return lax.all_to_all(jnp.broadcast_to(array[None], (size, *array.shape)), axes, 0, 0)


def body(grads):
    count, depth = grads.shape
    part = depth // 8
    za = lax.axis_index("za")

    held = lax.all_to_all(grads.reshape(count, 8, part).transpose(1, 0, 2), SUM, 0, 0)
    held = held.reshape(4, 2 * count, part)

    columns = lax.all_to_all(jnp.concatenate([held, held]), ("zh", "za"), 0, 0)
    columns = to_all(columns, "x", 4).reshape(2, 2, 16, count, part)
    columns = lax.all_to_all(columns.swapaxes(0, 1), "core", 0, 0)
    columns = columns.transpose(1, 2, 0, 3, 4).reshape(2, 32 * count, part)

    rows = held[:, None]
    for step in (2, 1):
        other = lax.ppermute(rows, "za", [(z, z ^ step) for z in range(4)])
        rows = jnp.stack([rows, other], axis=2).reshape(4, -1, 2 * count, part)
    rows = to_all(rows, "core", 2)
    rows = rows.swapaxes(0, 1).reshape(4, 16 * count, part)

    products = cross(rows.reshape(64 * count, part), columns.reshape(64 * count, part))
    products = products.reshape(4, 16 * count, 2, 32 * count).swapaxes(1, 2)
    extra = jnp.zeros((4, 2, 8, 32 * count), jnp.float32)
    extra = extra.at[:, :, 0, : 16 * count].set(squares(rows)[:, None])
    extra = extra.at[:, :, 1].set(squares(columns)[None])
    message = jnp.concatenate([products, extra], axis=2).reshape(8, -1, 32 * count)
    total = jnp.sum(lax.all_to_all(message, SUM, 0, 0), axis=0)
    left = lax.rsqrt(total[16 * count, : 16 * count] + 1e-06)
    right = lax.rsqrt(total[16 * count + 1] + 1e-06)
    gram = left[:, None] * total[: 16 * count] * right[None, :]

    gram = gram.reshape(2, 2, 2, 2, count, 32 * count)
    gram = swap(za >> 1, gram, 1)
    gram = swap(za & 1, gram, 2)
    return gram.transpose(1, 2, 3, 0, 4, 5).reshape(16 * count, 32 * count)


def solution(mesh):
    fine = Mesh(mesh.devices.reshape(SIZES), AXES)
    return jax.shard_map(
        body,
        mesh=fine,
        in_specs=(P(AXES, None),),
        out_specs=P(("y", "x", "zh"), ("za", "zb", "core")),
        check_vma=False,
    )
```

time: 1010 us -> 132 us (0.13)
  the two profiles are of different devices: /device:TPU:48 before, /device:TPU:1 now
where the time goes in v3:
time: 132 us
  blocking collectives  64.1 us (49%)
  waiting for transfers between devices  37.4 us (28%)
  starting transfers between devices  24.7 us (19%)
  other arithmetic  2.61 us (2%)
  local copies, waits for them, and re-layouts  1.82 us (1%)
    all_to_all x1, blocking collectives, body(): columns = lax.all_to_all(jnp.concatenate([held, held]), ('zh', 'za'), 0, 0)  32.1 us
    ppermute x2, starting transfers between devices, body(): other = lax.ppermute(rows, 'za', [(z, z ^ step) for z in range(4)])  17.2 us
    all_to_all x1, waiting for transfers between devices, body(): total = jnp.sum(lax.all_to_all(message, SUM, 0, 0), axis=0)  16.1 us
    all_to_all x1, blocking collectives, to_all(): lax.all_to_all(jnp.broadcast_to(array[None], (size, *array.shape)), axes,...  14.2 us
    all_to_all x1, waiting for transfers between devices, to_all(): lax.all_to_all(jnp.broadcast_to(array[None], (size, *array.shape)), axes,...  13.8 us
    all_to_all x1, blocking collectives, body(): lax.all_to_all(grads.reshape(count, 8, part).transpose(1, 0, 2), SUM, 0, 0)  11.9 us
    ppermute x2, waiting for transfers between devices, body(): other = lax.ppermute(rows, 'za', [(z, z ^ step) for z in range(4)])  7.48 us
    all_to_all x1, blocking collectives, body(): columns = lax.all_to_all(columns.swapaxes(0, 1), 'core', 0, 0)  5.94 us
  transfers between devices with their start and end apart: 4, of which 4 were waited for; matrix products, arithmetic and copies ran while one was open for 0% of the time, Pallas kernels for 0%

profile of v3, /device:TPU:1, one launch (start us, length us, event | category | flops | bytes accessed | tf_op | source)
XLA Modules:
  0.0 131.6 jit_solution(1403580317338331529)
XLA Ops:
  0.0 11.9 %all_to_all.30 = bf16[8,8,1024]{2,1,0:T(8,128)(2,1)S(1)} all-to-all(bf16[8,8,1024]{2,1,0:T(8,128)(2,1)} %bitcast.55), channel_id=1, replica_groups=mesh['y'=4,'x'=4,'zh'=2,'za'=4,'zb'=2,'core'=2] {'y','zb'}, dimensions={0} | all-to-all | bytes 262144 | tf_op jit(solution)/shard_map/all_to_all | solution.py:35
  11.9 8.8 %collective-permute-start = (bf16[4,1,16,1024]{3,2,0,1:T(8,128)(2,1)S(1)}, bf16[4,1,16,1024]{3,2,0,1:T(8,128)(2,1)S(1)}, u32[]{:S(2)}, u32[]{:S(2)}) collective-permute-start(bf16[4,1,16,1024]{3,2,0,1:T(8,128)(2,1)S(1)} %bitcast.48), channel_id=1, source_target_pairs={{0,8},{4,12},{8,0},{12,4},{1,9},{5,13},{9,1},{13,5},{2,10},{6,14},... | collective-permute-start | bytes 393224 | tf_op jit(solution)/shard_map/ppermute | solution.py:45
  20.8 3.8 %collective-permute-done = bf16[4,1,16,1024]{3,2,0,1:T(8,128)(2,1)S(1)} collective-permute-done((bf16[4,1,16,1024]{3,2,0,1:T(8,128)(2,1)S(1)}, bf16[4,1,16,1024]{3,2,0,1:T(8,128)(2,1)S(1)}, u32[]{:S(2)}, u32[]{:S(2)}) %collective-permute-start) | collective-permute-done | bytes 131104 | tf_op jit(solution)/shard_map/ppermute | solution.py:45
  24.6 8.3 %collective-permute-start.1 = (bf16[4,2,16,1024]{3,2,1,0:T(8,128)(2,1)S(1)}, bf16[4,2,16,1024]{3,2,1,0:T(8,128)(2,1)S(1)}, u32[]{:S(2)}, u32[]{:S(2)}) collective-permute-start(bf16[4,2,16,1024]{3,2,1,0:T(8,128)(2,1)S(1)} %get-tuple-element.30), channel_id=1, source_target_pairs={{0,4},{4,0},{8,12},{12,8},{1,5},{5,1},{9,13},{13,9},{2,6},{6,2},{1... | collective-permute-start | bytes 786440 | tf_op jit(solution)/shard_map/ppermute | solution.py:45
  32.9 3.7 %collective-permute-done.1 = bf16[4,2,16,1024]{3,2,1,0:T(8,128)(2,1)S(1)} collective-permute-done((bf16[4,2,16,1024]{3,2,1,0:T(8,128)(2,1)S(1)}, bf16[4,2,16,1024]{3,2,1,0:T(8,128)(2,1)S(1)}, u32[]{:S(2)}, u32[]{:S(2)}) %collective-permute-start.1) | collective-permute-done | bytes 262176 | tf_op jit(solution)/shard_map/ppermute | solution.py:45
  36.7 0.1 broadcast_in_dim.11
  36.8 14.2 %all_to_all.31 = bf16[2,4,4,16,1024]{4,3,2,1,0:T(8,128)(2,1)S(1)} all-to-all(bf16[2,4,4,16,1024]{4,3,2,1,0:T(8,128)(2,1)S(1)} %broadcast_in_dim.11), channel_id=1, replica_groups=mesh['y'=4,'x'=4,'zh'=2,'za'=4,'zb'=2,'core'=2] {'core'}, dimensions={0} | all-to-all | bytes 2097152 | tf_op jit(solution)/shard_map/all_to_all | solution.py:27
  51.0 32.1 %all_to_all.32 = bf16[8,16,1024]{2,1,0:T(8,128)(2,1)S(1)} all-to-all(bf16[8,16,1024]{2,1,0:T(8,128)(2,1)S(1)} %pad_maximum_fusion.3), channel_id=1, replica_groups=mesh['y'=4,'x'=4,'zh'=2,'za'=4,'zb'=2,'core'=2] {'zh','za'}, dimensions={0} | all-to-all | bytes 524288 | tf_op jit(solution)/shard_map/all_to_all | solution.py:38
  83.1 1.1 broadcast_in_dim.12
  84.2 4.0 %all-to-all-start.3 = ((bf16[4,8,16,1024]{3,2,1,0:T(8,128)(2,1)}), bf16[4,8,16,1024]{3,2,1,0:T(8,128)(2,1)S(1)}, u32[]{:S(2)}, u32[]{:S(2)}) async-start(bf16[4,8,16,1024]{3,2,1,0:T(8,128)(2,1)} %broadcast_in_dim.12), calls=%async_computation.3 | async-start | bytes 2097152 | tf_op jit(solution)/shard_map/all_to_all | solution.py:27
  88.3 0.3 multiply_reduce_fusion.1
  88.5 0.1 broadcast_in_dim.13
  88.6 0.1 copy.29
  88.8 13.8 %all-to-all-done.3 = bf16[4,8,16,1024]{3,2,1,0:T(8,128)(2,1)S(1)} async-done(((bf16[4,8,16,1024]{3,2,1,0:T(8,128)(2,1)}), bf16[4,8,16,1024]{3,2,1,0:T(8,128)(2,1)S(1)}, u32[]{:S(2)}, u32[]{:S(2)}) %all-to-all-start.3) | async-done | bytes 1048608 | tf_op jit(solution)/shard_map/all_to_all | solution.py:27
  102.7 5.9 %all_to_all.33 = bf16[2,2,16,8,1024]{4,3,2,1,0:T(8,128)(2,1)S(1)} all-to-all(bf16[2,2,16,8,1024]{4,3,2,1,0:T(8,128)(2,1)S(1)} %copy.30), channel_id=1, replica_groups=mesh['y'=4,'x'=4,'zh'=2,'za'=4,'zb'=2,'core'=2] {'core'}, dimensions={0} | all-to-all | bytes 2097152 | tf_op jit(solution)/shard_map/all_to_all | solution.py:40
  108.6 0.3 multiply_reduce_fusion
  108.9 0.1 broadcast_in_dim.14
  109.0 0.1 copy.31
  109.1 0.7 convolution_bitcast_fusion
  109.9 1.1 pad_maximum_fusion
  111.0 3.6 %all-to-all-start.5 = ((f32[8,136,256]{2,1,0:T(8,128)}), f32[8,136,256]{2,1,0:T(8,128)S(1)}, u32[]{:S(2)}, u32[]{:S(2)}) async-start(f32[8,136,256]{2,1,0:T(8,128)} %bitcast.22), calls=%async_computation.5 | async-start | bytes 2228224 | tf_op jit(solution)/shard_map/all_to_all | solution.py:56
  114.6 16.1 %all-to-all-done.5 = f32[8,136,256]{2,1,0:T(8,128)S(1)} async-done(((f32[8,136,256]{2,1,0:T(8,128)}), f32[8,136,256]{2,1,0:T(8,128)S(1)}, u32[]{:S(2)}, u32[]{:S(2)}) %all-to-all-start.5) | async-done | bytes 1114144 | tf_op jit(solution)/shard_map/all_to_all | solution.py:56
  130.8 0.1 fusion.2
  131.0 0.7 reverse_select_fusion
  (15 shorter events, 0.4 us)
Async XLA Ops:
  11.9 12.6 %collective-permute-start = (bf16[4,1,16,1024]{3,2,0,1:T(8,128)(2,1)S(1)}, bf16[4,1,16,1024]{3,2,0,1:T(8,128)(2,1)S(1)}, u32[]{:S(2)}, u32[]{:S(2)}) collective-permute-start(bf16[4,1,16,1024]{3,2,0,1:T(8,128)(2,1)S(1)} %bitcast.48), channel_id=1, source_target_pairs={{0,8},{4,12},{8,0},{12,4},{1,9},{5,13},{9,1},{13,5},{2,10},{6,14},... | collective-permute-start | bytes 393224 | tf_op jit(solution)/shard_map/ppermute | solution.py:45
  24.6 12.1 %collective-permute-start.1 = (bf16[4,2,16,1024]{3,2,1,0:T(8,128)(2,1)S(1)}, bf16[4,2,16,1024]{3,2,1,0:T(8,128)(2,1)S(1)}, u32[]{:S(2)}, u32[]{:S(2)}) collective-permute-start(bf16[4,2,16,1024]{3,2,1,0:T(8,128)(2,1)S(1)} %get-tuple-element.30), channel_id=1, source_target_pairs={{0,4},{4,0},{8,12},{12,8},{1,5},{5,1},{9,13},{13,9},{2,6},{6,2},{1... | collective-permute-start | bytes 786440 | tf_op jit(solution)/shard_map/ppermute | solution.py:45
  84.2 18.3 %all-to-all-start.3 = ((bf16[4,8,16,1024]{3,2,1,0:T(8,128)(2,1)}), bf16[4,8,16,1024]{3,2,1,0:T(8,128)(2,1)S(1)}, u32[]{:S(2)}, u32[]{:S(2)}) async-start(bf16[4,8,16,1024]{3,2,1,0:T(8,128)(2,1)} %broadcast_in_dim.12), calls=%async_computation.3 | async-start | bytes 2097152 | tf_op jit(solution)/shard_map/all_to_all | solution.py:27
  111.0 19.7 %all-to-all-start.5 = ((f32[8,136,256]{2,1,0:T(8,128)}), f32[8,136,256]{2,1,0:T(8,128)S(1)}, u32[]{:S(2)}, u32[]{:S(2)}) async-start(f32[8,136,256]{2,1,0:T(8,128)} %bitcast.22), calls=%async_computation.5 | async-start | bytes 2228224 | tf_op jit(solution)/shard_map/all_to_all | solution.py:56

commit v4 on v1

v4 whole, which is shorter than its diff:
```python
import jax
import jax.numpy as jnp
from jax import lax
from jax.sharding import Mesh, PartitionSpec as P

AXES = ("y", "x", "zh", "zl", "core")
SIZES = (4, 4, 2, 8, 2)
Z = ("zh", "zl")


def squares(block):
    wide = block.astype(jnp.float32)
    return jnp.sum(wide * wide, axis=-1)


def cross(left, right):
    return lax.dot_general(
        left, right, (((1,), (1,)), ((), ())), preferred_element_type=jnp.float32
    )


def linear(y, x, z, core):
    return ((y * 4 + x) * 16 + z) * 2 + core


def spread(flip):
    pairs = []
    for y in range(4):
        for x in range(4):
            for z in range(16):
                for core in range(2):
                    plane = (core ^ flip) * 8 + 2 * y + x // 2
                    pairs.append((linear(y, x, z, core), linear(y ^ z // 4, x ^ z % 4, plane, x % 2)))
    return pairs


def swap(flag, array, axis):
    return jnp.where(flag == 1, jnp.flip(array, axis), array)


def to_all(array, axes):
    return lax.all_to_all(jnp.broadcast_to(array[None], (4, *array.shape)), axes, 0, 0)


def body(grads):
    count, depth = grads.shape
    half = depth // 2
    zh, zl, core = (lax.axis_index(a) for a in ("zh", "zl", "core"))

    first = lax.ppermute(grads, AXES, spread(0))
    second = lax.ppermute(grads, AXES, spread(1))
    mine = jnp.where(zh == 0, jnp.concatenate([first, second]), jnp.concatenate([second, first]))
    low = to_all(to_all(mine[:, :half], "y"), "x")
    high = to_all(to_all(mine[:, half:], "x"), "y")

    rows = grads[None]
    for step in (4, 2, 1):
        other = lax.ppermute(rows, Z, [(z, z ^ step) for z in range(16)])
        rows = jnp.stack([rows, other], axis=1 if step != 4 else 0).reshape(-1, *grads.shape)
    rows = rows.reshape(8 * count, depth)
    other = lax.ppermute(rows, "core", [(0, 1), (1, 0)])
    rows = jnp.concatenate([rows, other])

    size = 2 * count
    low_part = cross(low.reshape(16 * size, half), rows[:, :half]).reshape(4, 4, size, -1)
    high_part = cross(high.reshape(16 * size, half), rows[:, half:]).reshape(4, 4, size, -1)
    gram = low_part.swapaxes(0, 1) + high_part
    right = lax.rsqrt(squares(low).swapaxes(0, 1) + squares(high) + 1e-06)
    left = lax.rsqrt(squares(rows) + 1e-06)
    gram = gram * right[..., None] * left
    gram = gram.reshape(2, 2, 2, 2, size, -1)
    for axis, flag in ((0, zl >> 2 & 1), (1, zl >> 1 & 1), (2, zl & 1), (3, core)):
        gram = swap(flag, gram, axis)
    gram = gram.reshape(16 * size, -1).T.reshape(2, 2, 2, 2, count, -1)
    for axis, flag in ((0, core), (1, zl >> 2 & 1), (2, zl >> 1 & 1), (3, zl & 1)):
        gram = swap(flag, gram, axis)
    return gram.transpose(1, 2, 3, 0, 4, 5).reshape(16 * count, -1)


def solution(mesh):
    fine = Mesh(mesh.devices.reshape(SIZES), AXES)
    return jax.shard_map(
        body, mesh=fine, in_specs=(P(AXES, None),), out_specs=P(("y", "x", "zh"), ("zl", "core")), check_vma=False
    )
```

time: 151 us -> 138 us (0.914)
  the two profiles are of different devices: /device:TPU:2 before, /device:TPU:288 now
where the time goes in v4:
time: 138 us; the launch traced here: 137 us
  waiting for transfers between devices  67.4 us (49%)
  starting transfers between devices  54.3 us (39%)
  local copies, waits for them, and re-layouts  6.67 us (5%)
  other arithmetic  4.63 us (3%)
  matrix products  4.13 us (3%)
    all_to_all x4, waiting for transfers between devices, to_all(): lax.all_to_all(jnp.broadcast_to(array[None], (4, *array.shape)), axes, 0, 0)  40.1 us
    all_to_all x4, starting transfers between devices, to_all(): lax.all_to_all(jnp.broadcast_to(array[None], (4, *array.shape)), axes, 0, 0)  26.5 us
    ppermute x3, starting transfers between devices, body(): other = lax.ppermute(rows, Z, [(z, z ^ step) for z in range(16)])  17.4 us
    ppermute x1, waiting for transfers between devices, body(): first = lax.ppermute(grads, AXES, spread(0))  12.8 us
    ppermute x3, waiting for transfers between devices, body(): other = lax.ppermute(rows, Z, [(z, z ^ step) for z in range(16)])  11.9 us
    ppermute x1, starting transfers between devices, body(): second = lax.ppermute(grads, AXES, spread(1))  6.46 us
    broadcast_in_dim x4, local copies, waits for them, and re-layouts, to_all(): jnp.broadcast_to(array[None], (4, *array.shape))  5.87 us
    reduce_sum x3, other arithmetic, squares(): return jnp.sum(wide * wide, axis=-1)  4.25 us
  transfers between devices with their start and end apart: 10, of which 6 were waited for; matrix products, arithmetic and copies ran while one was open for 5% of the time, Pallas kernels for 0%

profile of v4, /device:TPU:288, one launch (start us, length us, event | category | flops | bytes accessed | tf_op | source)
XLA Modules:
  0.0 137.4 jit_solution(4377862260596331972)
XLA Ops:
  0.0 2.1 %collective-permute-start = (bf16[8,8192]{1,0:T(8,128)(2,1)}, bf16[8,8192]{1,0:T(8,128)(2,1)S(1)}, u32[]{:S(2)}, u32[]{:S(2)}) collective-permute-start(bf16[8,8192]{1,0:T(8,128)(2,1)} %param.1), channel_id=1, source_target_pairs={{0,0},{1,16},{2,32},{3,48},{4,64},{5,80},{6,96},{7,112},{8,128},{9... | collective-permute-start | bytes 393224 | tf_op jit(solution)/shard_map/ppermute | solution.py:50
  2.1 6.5 %collective-permute-start.1 = (bf16[8,8192]{1,0:T(8,128)(2,1)}, bf16[8,8192]{1,0:T(8,128)(2,1)S(1)}, u32[]{:S(2)}, u32[]{:S(2)}) collective-permute-start(bf16[8,8192]{1,0:T(8,128)(2,1)} %param.1), channel_id=1, source_target_pairs={{0,16},{1,0},{2,48},{3,32},{4,80},{5,64},{6,112},{7,96},{8,144},{9... | collective-permute-start | bytes 393224 | tf_op jit(solution)/shard_map/ppermute | solution.py:51
  8.5 12.8 %collective-permute-done = bf16[8,8192]{1,0:T(8,128)(2,1)S(1)} collective-permute-done((bf16[8,8192]{1,0:T(8,128)(2,1)}, bf16[8,8192]{1,0:T(8,128)(2,1)S(1)}, u32[]{:S(2)}, u32[]{:S(2)}) %collective-permute-start) | collective-permute-done | bytes 131104 | tf_op jit(solution)/shard_map/ppermute | solution.py:50
  21.4 2.6 %collective-permute-done.1 = bf16[8,8192]{1,0:T(8,128)(2,1)S(1)} collective-permute-done((bf16[8,8192]{1,0:T(8,128)(2,1)}, bf16[8,8192]{1,0:T(8,128)(2,1)S(1)}, u32[]{:S(2)}, u32[]{:S(2)}) %collective-permute-start.1) | collective-permute-done | bytes 131104 | tf_op jit(solution)/shard_map/ppermute | solution.py:51
  24.1 0.8 broadcast_in_dim.13
  24.9 3.5 %all-to-all-start.2 = ((bf16[4,16,4096]{2,1,0:T(8,128)(2,1)}), bf16[4,16,4096]{2,1,0:T(8,128)(2,1)S(1)}, u32[]{:S(2)}, u32[]{:S(2)}) async-start(bf16[4,16,4096]{2,1,0:T(8,128)(2,1)} %broadcast_in_dim.13), calls=%async_computation.2 | async-start | bytes 1048576 | tf_op jit(solution)/shard_map/all_to_all | solution.py:42
  28.4 12.3 %collective-permute-start.2 = (bf16[1,8,8192]{2,1,0:T(8,128)(2,1)S(1)}, bf16[1,8,8192]{2,1,0:T(8,128)(2,1)S(1)}, u32[]{:S(2)}, u32[]{:S(2)}) collective-permute-start(bf16[1,8,8192]{2,1,0:T(8,128)(2,1)S(1)} %bitcast.52), channel_id=1, source_target_pairs={{0,8},{2,10},{4,12},{6,14},{8,0},{10,2},{12,4},{14,6},{16,24},{18,... | collective-permute-start | bytes 393224 | tf_op jit(solution)/shard_map/ppermute | solution.py:58
  40.7 0.8 broadcast_in_dim.10
  41.5 14.9 %all-to-all-start = ((bf16[4,16,4096]{2,1,0:T(8,128)(2,1)}), bf16[4,16,4096]{2,1,0:T(8,128)(2,1)S(1)}, u32[]{:S(2)}, u32[]{:S(2)}) async-start(bf16[4,16,4096]{2,1,0:T(8,128)(2,1)} %broadcast_in_dim.10), calls=%async_computation | async-start | bytes 1048576 | tf_op jit(solution)/shard_map/all_to_all | solution.py:42
  56.5 1.9 %collective-permute-start.3 = (bf16[2,8,8192]{2,1,0:T(8,128)(2,1)S(1)}, bf16[2,8,8192]{2,1,0:T(8,128)(2,1)S(1)}, u32[]{:S(2)}, u32[]{:S(2)}) collective-permute-start(bf16[2,8,8192]{2,1,0:T(8,128)(2,1)S(1)} %maximum_bitcast_fusion), channel_id=1, source_target_pairs={{0,4},{2,6},{4,0},{6,2},{8,12},{10,14},{12,8},{14,10},{16,20},{18,... | collective-permute-start | bytes 786440 | tf_op jit(solution)/shard_map/ppermute | solution.py:58
  58.4 8.1 %all-to-all-done = bf16[4,16,4096]{2,1,0:T(8,128)(2,1)S(1)} async-done(((bf16[4,16,4096]{2,1,0:T(8,128)(2,1)}), bf16[4,16,4096]{2,1,0:T(8,128)(2,1)S(1)}, u32[]{:S(2)}, u32[]{:S(2)}) %all-to-all-start) | async-done | bytes 524320 | tf_op jit(solution)/shard_map/all_to_all | solution.py:42
  66.6 1.6 %broadcast_in_dim.14 = bf16[4,4,16,4096]{3,2,1,0:T(8,128)(2,1)} broadcast(bf16[4,16,4096]{2,1,0:T(8,128)(2,1)S(1)} %all-to-all-done.2), dimensions={1,2,3} | broadcast | bytes 2621440 | tf_op jit(solution)/shard_map/broadcast_in_dim | solution.py:42
  68.1 3.6 %all-to-all-start.3 = ((bf16[4,4,16,4096]{3,2,1,0:T(8,128)(2,1)}), bf16[4,4,16,4096]{3,2,1,0:T(8,128)(2,1)S(1)}, u32[]{:S(2)}, u32[]{:S(2)}) async-start(bf16[4,4,16,4096]{3,2,1,0:T(8,128)(2,1)} %broadcast_in_dim.14), calls=%async_computation.3 | async-start | bytes 4194304 | tf_op jit(solution)/shard_map/all_to_all | solution.py:42
  71.8 3.2 %collective-permute-start.4 = (bf16[4,8,8192]{2,1,0:T(8,128)(2,1)S(1)}, bf16[4,8,8192]{2,1,0:T(8,128)(2,1)S(1)}, u32[]{:S(2)}, u32[]{:S(2)}) collective-permute-start(bf16[4,8,8192]{2,1,0:T(8,128)(2,1)S(1)} %bitcast.47), channel_id=1, source_target_pairs={{0,2},{2,0},{4,6},{6,4},{8,10},{10,8},{12,14},{14,12},{16,18},{18,... | collective-permute-start | bytes 1572872 | tf_op jit(solution)/shard_map/ppermute | solution.py:58
  75.0 11.9 %collective-permute-done.4 = bf16[4,8,8192]{2,1,0:T(8,128)(2,1)S(1)} collective-permute-done((bf16[4,8,8192]{2,1,0:T(8,128)(2,1)S(1)}, bf16[4,8,8192]{2,1,0:T(8,128)(2,1)S(1)}, u32[]{:S(2)}, u32[]{:S(2)}) %collective-permute-start.4) | collective-permute-done | bytes 524320 | tf_op jit(solution)/shard_map/ppermute | solution.py:58
  87.0 1.9 %collective-permute-start.5 = (bf16[64,8192]{1,0:T(8,128)(2,1)S(1)}, bf16[64,8192]{1,0:T(8,128)(2,1)}, u32[]{:S(2)}, u32[]{:S(2)}) collective-permute-start(bf16[64,8192]{1,0:T(8,128)(2,1)S(1)} %bitcast.43), channel_id=1, source_target_pairs={{0,1},{1,0},{2,3},{3,2},{4,5},{5,4},{6,7},{7,6},{8,9},{9,8},{10,11... | collective-permute-start | bytes 3145736 | tf_op jit(solution)/shard_map/ppermute | solution.py:61
  88.9 8.9 %all-to-all-done.3 = bf16[4,4,16,4096]{3,2,1,0:T(8,128)(2,1)S(1)} async-done(((bf16[4,4,16,4096]{3,2,1,0:T(8,128)(2,1)}), bf16[4,4,16,4096]{3,2,1,0:T(8,128)(2,1)S(1)}, u32[]{:S(2)}, u32[]{:S(2)}) %all-to-all-start.3) | async-done | bytes 2097184 | tf_op jit(solution)/shard_map/all_to_all | solution.py:42
  97.8 2.6 %broadcast_in_dim.11 = bf16[4,4,16,4096]{3,2,1,0:T(8,128)(2,1)} broadcast(bf16[4,16,4096]{2,1,0:T(8,128)(2,1)} %copy-done), dimensions={1,2,3} | broadcast | bytes 2621440 | tf_op jit(solution)/shard_map/broadcast_in_dim | solution.py:42
  100.5 4.5 %all-to-all-start.1 = ((bf16[4,4,16,4096]{3,2,1,0:T(8,128)(2,1)}), bf16[4,4,16,4096]{3,2,1,0:T(8,128)(2,1)}, u32[]{:S(2)}, u32[]{:S(2)}) async-start(bf16[4,4,16,4096]{3,2,1,0:T(8,128)(2,1)} %broadcast_in_dim.11), calls=%async_computation.1 | async-start | bytes 4194304 | tf_op jit(solution)/shard_map/all_to_all | solution.py:42
  105.0 1.7 %multiply_reduce_fusion = f32[128]{0:T(128)S(1)} fusion(bf16[64,8192]{1,0:T(8,128)(2,1)} %collective-permute-done.5, bf16[64,8192]{1,0:T(8,128)(2,1)S(1)} %bitcast.44), kind=kLoop, calls=%fused_computation | loop fusion | flops 6291328 | bytes 2097664 | tf_op jit(solution)/shard_map/reduce_sum | solution.py:13
  107.2 23.0 %all-to-all-done.1 = bf16[4,4,16,4096]{3,2,1,0:T(8,128)(2,1)} async-done(((bf16[4,4,16,4096]{3,2,1,0:T(8,128)(2,1)}), bf16[4,4,16,4096]{3,2,1,0:T(8,128)(2,1)}, u32[]{:S(2)}, u32[]{:S(2)}) %all-to-all-start.1) | async-done | bytes 2097184 | tf_op jit(solution)/shard_map/all_to_all | solution.py:42
  130.2 2.1 %multiply_reduce_fusion.2 = f32[4,4,16]{2,1,0:T(4,128)S(1)} fusion(bf16[4,4,16,4096]{3,2,1,0:T(8,128)(2,1)} %all-to-all-done.1), kind=kLoop, calls=%fused_computation.2 | loop fusion | flops 3145472 | bytes 2098176 | tf_op jit(solution)/shard_map/reduce_sum | solution.py:13
  132.3 1.7 %fusion = f32[4,4,16,128]{3,2,0,1:T(8,128)S(1)} fusion(bf16[4,4,16,4096]{3,2,1,0:T(8,128)(2,1)S(1)} %all-to-all-done.3, bf16[64,8192]{1,0:T(8,128)(2,1)S(1)} %bitcast.45, bf16[64,8192]{1,0:T(8,128)(2,1)} %collective-permute-done.5), kind=kOutput, calls=%fused_computation.8 | convolution fusion | flops 270532608 | bytes 4325376 | tf_op jit(solution)/shard_map/dot_general | solution.py:17
  134.1 2.4 %fusion.4 = f32[4,4,16,128]{3,2,0,1:T(8,128)S(1)} fusion(f32[4,4,16,128]{3,2,0,1:T(8,128)S(1)} %fusion, bf16[4,4,16,4096]{3,2,1,0:T(8,128)(2,1)} %all-to-all-done.1, bf16[64,8192]{1,0:T(8,128)(2,1)S(1)} %bitcast.46, bf16[64,8192]{1,0:T(8,128)(2,1)} %collective-permute-done.5, f32[128]{0:T(128)S(1)} %add_rsqrt_fusion, f32[4,4,16]{2,0,1:T(4,128)S(1)} %fusion.13), kind=kOutput, calls=%fused_computation.13 | convolution fusion | flops 270630912 | bytes 4457984 | tf_op jit(solution)/shard_map/dot_general | solution.py:17
  (27 shorter events, 1.7 us)
Async XLA Ops:
  0.0 28.4 %copy-start.1 = (bf16[8,8192]{1,0:T(8,128)(2,1)S(1)}, bf16[8,8192]{1,0:T(8,128)(2,1)}, u32[]{:S(2)}) copy-start(bf16[8,8192]{1,0:T(8,128)(2,1)} %param.1) | copy-start | bytes 393220
  0.0 21.4 %collective-permute-start = (bf16[8,8192]{1,0:T(8,128)(2,1)}, bf16[8,8192]{1,0:T(8,128)(2,1)S(1)}, u32[]{:S(2)}, u32[]{:S(2)}) collective-permute-start(bf16[8,8192]{1,0:T(8,128)(2,1)} %param.1), channel_id=1, source_target_pairs={{0,0},{1,16},{2,32},{3,48},{4,64},{5,80},{6,96},{7,112},{8,128},{9... | collective-permute-start | bytes 393224 | tf_op jit(solution)/shard_map/ppermute | solution.py:50
  2.1 21.9 %collective-permute-start.1 = (bf16[8,8192]{1,0:T(8,128)(2,1)}, bf16[8,8192]{1,0:T(8,128)(2,1)S(1)}, u32[]{:S(2)}, u32[]{:S(2)}) collective-permute-start(bf16[8,8192]{1,0:T(8,128)(2,1)} %param.1), channel_id=1, source_target_pairs={{0,16},{1,0},{2,48},{3,32},{4,80},{5,64},{6,112},{7,96},{8,144},{9... | collective-permute-start | bytes 393224 | tf_op jit(solution)/shard_map/ppermute | solution.py:51
  24.9 15.8 %all-to-all-start.2 = ((bf16[4,16,4096]{2,1,0:T(8,128)(2,1)}), bf16[4,16,4096]{2,1,0:T(8,128)(2,1)S(1)}, u32[]{:S(2)}, u32[]{:S(2)}) async-start(bf16[4,16,4096]{2,1,0:T(8,128)(2,1)} %broadcast_in_dim.13), calls=%async_computation.2 | async-start | bytes 1048576 | tf_op jit(solution)/shard_map/all_to_all | solution.py:42
  28.4 28.1 %collective-permute-start.2 = (bf16[1,8,8192]{2,1,0:T(8,128)(2,1)S(1)}, bf16[1,8,8192]{2,1,0:T(8,128)(2,1)S(1)}, u32[]{:S(2)}, u32[]{:S(2)}) collective-permute-start(bf16[1,8,8192]{2,1,0:T(8,128)(2,1)S(1)} %bitcast.52), channel_id=1, source_target_pairs={{0,8},{2,10},{4,12},{6,14},{8,0},{10,2},{12,4},{14,6},{16,24},{18,... | collective-permute-start | bytes 393224 | tf_op jit(solution)/shard_map/ppermute | solution.py:58
  41.5 25.0 %all-to-all-start = ((bf16[4,16,4096]{2,1,0:T(8,128)(2,1)}), bf16[4,16,4096]{2,1,0:T(8,128)(2,1)S(1)}, u32[]{:S(2)}, u32[]{:S(2)}) async-start(bf16[4,16,4096]{2,1,0:T(8,128)(2,1)} %broadcast_in_dim.10), calls=%async_computation | async-start | bytes 1048576 | tf_op jit(solution)/shard_map/all_to_all | solution.py:42
  56.5 15.2 %collective-permute-start.3 = (bf16[2,8,8192]{2,1,0:T(8,128)(2,1)S(1)}, bf16[2,8,8192]{2,1,0:T(8,128)(2,1)S(1)}, u32[]{:S(2)}, u32[]{:S(2)}) collective-permute-start(bf16[2,8,8192]{2,1,0:T(8,128)(2,1)S(1)} %maximum_bitcast_fusion), channel_id=1, source_target_pairs={{0,4},{2,6},{4,0},{6,2},{8,12},{10,14},{12,8},{14,10},{16,20},{18,... | collective-permute-start | bytes 786440 | tf_op jit(solution)/shard_map/ppermute | solution.py:58
  66.6 1.6 %copy-start = (bf16[4,16,4096]{2,1,0:T(8,128)(2,1)}, bf16[4,16,4096]{2,1,0:T(8,128)(2,1)S(1)}, u32[]{:S(2)}) copy-start(bf16[4,16,4096]{2,1,0:T(8,128)(2,1)S(1)} %all-to-all-done) | copy-start | bytes 1572868
  68.1 29.7 %all-to-all-start.3 = ((bf16[4,4,16,4096]{3,2,1,0:T(8,128)(2,1)}), bf16[4,4,16,4096]{3,2,1,0:T(8,128)(2,1)S(1)}, u32[]{:S(2)}, u32[]{:S(2)}) async-start(bf16[4,4,16,4096]{3,2,1,0:T(8,128)(2,1)} %broadcast_in_dim.14), calls=%async_computation.3 | async-start | bytes 4194304 | tf_op jit(solution)/shard_map/all_to_all | solution.py:42
  71.8 15.1 %collective-permute-start.4 = (bf16[4,8,8192]{2,1,0:T(8,128)(2,1)S(1)}, bf16[4,8,8192]{2,1,0:T(8,128)(2,1)S(1)}, u32[]{:S(2)}, u32[]{:S(2)}) collective-permute-start(bf16[4,8,8192]{2,1,0:T(8,128)(2,1)S(1)} %bitcast.47), channel_id=1, source_target_pairs={{0,2},{2,0},{4,6},{6,4},{8,10},{10,8},{12,14},{14,12},{16,18},{18,... | collective-permute-start | bytes 1572872 | tf_op jit(solution)/shard_map/ppermute | solution.py:58
  87.0 18.0 %collective-permute-start.5 = (bf16[64,8192]{1,0:T(8,128)(2,1)S(1)}, bf16[64,8192]{1,0:T(8,128)(2,1)}, u32[]{:S(2)}, u32[]{:S(2)}) collective-permute-start(bf16[64,8192]{1,0:T(8,128)(2,1)S(1)} %bitcast.43), channel_id=1, source_target_pairs={{0,1},{1,0},{2,3},{3,2},{4,5},{5,4},{6,7},{7,6},{8,9},{9,8},{10,11... | collective-permute-start | bytes 3145736 | tf_op jit(solution)/shard_map/ppermute | solution.py:61
  100.5 29.7 %all-to-all-start.1 = ((bf16[4,4,16,4096]{3,2,1,0:T(8,128)(2,1)}), bf16[4,4,16,4096]{3,2,1,0:T(8,128)(2,1)}, u32[]{:S(2)}, u32[]{:S(2)}) async-start(bf16[4,4,16,4096]{3,2,1,0:T(8,128)(2,1)} %broadcast_in_dim.11), calls=%async_computation.1 | async-start | bytes 4194304 | tf_op jit(solution)/shard_map/all_to_all | solution.py:42

commit v5 on v4

v5 whole, which is shorter than its diff:
```python
import jax
import jax.numpy as jnp
from jax import lax
from jax.sharding import Mesh, PartitionSpec as P

AXES = ("y", "xh", "xl", "zh", "zl", "core")
SIZES = (4, 2, 2, 2, 8, 2)
PLANE = ("y", "xh")
Z = ("zh", "zl")
TRADE = [(0, 1), (1, 0)]


def squares(block):
    wide = block.astype(jnp.float32)
    return jnp.sum(wide * wide, axis=-1)


def cross(left, right):
    return lax.dot_general(
        left, right, (((1,), (1,)), ((), ())), preferred_element_type=jnp.float32
    )


def linear(plane, xl, z, core):
    return ((plane * 2 + xl) * 16 + z) * 2 + core


def spread(part, away):
    pairs = []
    for plane in range(8):
        for xl in range(2):
            for zh in range(2):
                for zl in range(8):
                    for core in range(2):
                        target = linear(plane ^ zl, zh ^ part, (core ^ away) * 8 + plane, xl)
                        pairs.append((linear(plane, xl, zh * 8 + zl, core), target))
    return pairs


def swap(flag, array, axis):
    return jnp.where(flag == 1, jnp.flip(array, axis), array)


def body(grads):
    count, depth = grads.shape
    half = depth // 2
    zh, zl, core, xl = (lax.axis_index(a) for a in ("zh", "zl", "core", "xl"))
    low, high = grads[:, :half], grads[:, half:]

    near, far = jnp.where(zh == 0, low, high), jnp.where(zh == 0, high, low)
    sent = [lax.ppermute((near, far)[part], AXES, spread(part, away)) for part in (0, 1) for away in (0, 1)]
    mine = jnp.stack(sent)
    columns = lax.all_to_all(jnp.broadcast_to(mine[None], (8, *mine.shape)), PLANE, 0, 0)
    columns = columns.reshape(32 * count, half)

    keep, give = jnp.where(xl == 0, low, high), jnp.where(xl == 0, high, low)
    rows = jnp.stack([keep, lax.ppermute(give, "xl", TRADE)])[:, None]
    for step in (4, 2, 1):
        other = lax.ppermute(rows, Z, [(z, z ^ step) for z in range(16)])
        rows = jnp.stack([rows, other], axis=2).reshape(2, -1, count, half)
    other = lax.ppermute(rows, "core", TRADE)
    rows = jnp.stack([rows, other], axis=1).reshape(2, 16 * count, half)

    lengths = squares(columns)
    trade = lambda array: jnp.flip(array.reshape(8, 2, 2 * count, -1), 1).reshape(array.shape)
    extra = jnp.zeros((2, 8, 16 * count), jnp.float32)
    extra = extra.at[:, 0].set(squares(rows)).at[0, 1:3].set(lengths.reshape(2, -1))
    extra = extra.at[1, 1:3].set(trade(lengths[:, None]).reshape(2, -1))
    own = jnp.concatenate([cross(columns, rows[0]), extra[0]])
    other = jnp.concatenate([trade(cross(columns, rows[1])), extra[1]])
    total = own + lax.ppermute(other, "xl", TRADE)
    gram, extra = total[: 32 * count], lax.rsqrt(total[32 * count :] + 1e-06)
    gram = gram * extra[1:3].reshape(-1)[:, None] * extra[0]

    gram = gram.reshape(2, 2, 2, 2, 2, count, -1)
    for axis, flag in ((0, zl >> 2 & 1), (1, zl >> 1 & 1), (2, zl & 1), (3, xl), (4, zh)):
        gram = swap(flag, gram, axis)
    gram = gram.transpose(3, 0, 1, 2, 4, 5, 6).reshape(32 * count, -1).T.reshape(2, 2, 2, 2, count, -1)
    for axis, flag in ((0, core), (1, zl >> 2 & 1), (2, zl >> 1 & 1), (3, zl & 1)):
        gram = swap(flag, gram, axis)
    return gram.transpose(1, 2, 3, 0, 4, 5).reshape(16 * count, -1)


def solution(mesh):
    fine = Mesh(mesh.devices.reshape(SIZES), AXES)
    return jax.shard_map(
        body, mesh=fine, in_specs=(P(AXES, None),), out_specs=P(("y", "xh", "xl", "zh"), ("zl", "core")), check_vma=False
    )
```

time: 138 us -> 111 us (0.80)
  the two profiles are of different devices: /device:TPU:288 before, /device:TPU:1 now
where the time goes in v5:
time: 111 us; the launch traced here: 109 us
  starting transfers between devices  75.7 us (68%)
  waiting for transfers between devices  19.1 us (17%)
  other arithmetic  6.33 us (6%)
  local copies, waits for them, and re-layouts  5.01 us (5%)
  matrix products  2.63 us (2%)
    ppermute x4, starting transfers between devices, body(): lax.ppermute((near, far)[part], AXES, spread(part, away))  30 us
    all_to_all x1, starting transfers between devices, body(): lax.all_to_all(jnp.broadcast_to(mine[None], (8, *mine.shape)), PLANE, 0, 0)  14.5 us
    ppermute x3, starting transfers between devices, body(): other = lax.ppermute(rows, Z, [(z, z ^ step) for z in range(16)])  14.5 us
    ppermute x3, waiting for transfers between devices, body(): other = lax.ppermute(rows, Z, [(z, z ^ step) for z in range(16)])  11.4 us
    ppermute x1, starting transfers between devices, body(): total = own + lax.ppermute(other, 'xl', TRADE)  7.54 us
    ppermute x1, starting transfers between devices, body(): other = lax.ppermute(rows, 'core', TRADE)  5.22 us
    all_to_all x1, waiting for transfers between devices, body(): lax.all_to_all(jnp.broadcast_to(mine[None], (8, *mine.shape)), PLANE, 0, 0)  4.38 us
    ppermute x1, starting transfers between devices, body(): rows = jnp.stack([keep, lax.ppermute(give, 'xl', TRADE)])[:, None]  3.95 us
  transfers between devices with their start and end apart: 11, of which 5 were waited for; matrix products, arithmetic and copies ran while one was open for 4% of the time, Pallas kernels for 0%

profile of v5, /device:TPU:1, one launch (start us, length us, event | category | flops | bytes accessed | tf_op | source)
XLA Modules:
  0.0 109.2 jit_solution(3322813381230621863)
XLA Ops:
  0.0 0.9 broadcast_select_fusion.2
  0.9 3.9 %collective-permute-start.4 = (bf16[8,4096]{1,0:T(8,128)(2,1)S(1)}, bf16[8,4096]{1,0:T(8,128)(2,1)S(1)}, u32[]{:S(2)}, u32[]{:S(2)}) collective-permute-start(bf16[8,4096]{1,0:T(8,128)(2,1)S(1)} %get-tuple-element.47), channel_id=1, source_target_pairs={{0,32},{32,0},{1,33},{33,1},{2,34},{34,2},{3,35},{35,3},{4,36},{36... | collective-permute-start | bytes 196616 | tf_op jit(solution)/shard_map/ppermute | solution.py:57
  4.9 1.6 %collective-permute-done.4 = bf16[8,4096]{1,0:T(8,128)(2,1)S(1)} collective-permute-done((bf16[8,4096]{1,0:T(8,128)(2,1)S(1)}, bf16[8,4096]{1,0:T(8,128)(2,1)S(1)}, u32[]{:S(2)}, u32[]{:S(2)}) %collective-permute-start.4) | collective-permute-done | bytes 65568 | tf_op jit(solution)/shard_map/ppermute | solution.py:57
  6.5 9.1 %collective-permute-start.5 = (bf16[2,1,8,4096]{3,2,0,1:T(8,128)(2,1)S(1)}, bf16[2,1,8,4096]{3,2,0,1:T(8,128)(2,1)S(1)}, u32[]{:S(2)}, u32[]{:S(2)}) collective-permute-start(bf16[2,1,8,4096]{3,2,0,1:T(8,128)(2,1)S(1)} %get-tuple-element.50), channel_id=1, source_target_pairs={{0,8},{2,10},{4,12},{6,14},{8,0},{10,2},{12,4},{14,6},{16,24},{18,... | collective-permute-start | bytes 393224 | tf_op jit(solution)/shard_map/ppermute | solution.py:59
  15.6 5.1 %collective-permute-start.3 = (bf16[8,4096]{1,0:T(8,128)(2,1)S(1)}, bf16[8,4096]{1,0:T(8,128)(2,1)S(1)}, u32[]{:S(2)}, u32[]{:S(2)}) collective-permute-start(bf16[8,4096]{1,0:T(8,128)(2,1)S(1)} %get-tuple-element.48), channel_id=1, source_target_pairs={{0,48},{1,32},{2,112},{3,96},{4,176},{5,160},{6,240},{7,224},{8,30... | collective-permute-start | bytes 196616 | tf_op jit(solution)/shard_map/ppermute | solution.py:51
  20.7 10.4 %collective-permute-start.2 = (bf16[8,4096]{1,0:T(8,128)(2,1)S(1)}, bf16[8,4096]{1,0:T(8,128)(2,1)S(1)}, u32[]{:S(2)}, u32[]{:S(2)}) collective-permute-start(bf16[8,4096]{1,0:T(8,128)(2,1)S(1)} %get-tuple-element.48), channel_id=1, source_target_pairs={{0,32},{1,48},{2,96},{3,112},{4,160},{5,176},{6,224},{7,240},{8,28... | collective-permute-start | bytes 196616 | tf_op jit(solution)/shard_map/ppermute | solution.py:51
  31.1 2.3 %collective-permute-start.1 = (bf16[8,4096]{1,0:T(8,128)(2,1)S(1)}, bf16[8,4096]{1,0:T(8,128)(2,1)S(1)}, u32[]{:S(2)}, u32[]{:S(2)}) collective-permute-start(bf16[8,4096]{1,0:T(8,128)(2,1)S(1)} %get-tuple-element.45), channel_id=1, source_target_pairs={{0,16},{1,0},{2,80},{3,64},{4,144},{5,128},{6,208},{7,192},{8,272}... | collective-permute-start | bytes 196616 | tf_op jit(solution)/shard_map/ppermute | solution.py:51
  33.4 12.3 %collective-permute-start = (bf16[8,4096]{1,0:T(8,128)(2,1)S(1)}, bf16[8,4096]{1,0:T(8,128)(2,1)S(1)}, u32[]{:S(2)}, u32[]{:S(2)}) collective-permute-start(bf16[8,4096]{1,0:T(8,128)(2,1)S(1)} %get-tuple-element.45), channel_id=1, source_target_pairs={{0,0},{1,16},{2,64},{3,80},{4,128},{5,144},{6,192},{7,208},{8,256}... | collective-permute-start | bytes 196616 | tf_op jit(solution)/shard_map/ppermute | solution.py:51
  45.7 2.2 %collective-permute-start.6 = (bf16[2,2,8,4096]{3,2,1,0:T(8,128)(2,1)S(1)}, bf16[2,2,8,4096]{3,2,1,0:T(8,128)(2,1)S(1)}, u32[]{:S(2)}, u32[]{:S(2)}) collective-permute-start(bf16[2,2,8,4096]{3,2,1,0:T(8,128)(2,1)S(1)} %get-tuple-element.44), channel_id=1, source_target_pairs={{0,4},{2,6},{4,0},{6,2},{8,12},{10,14},{12,8},{14,10},{16,20},{18,... | collective-permute-start | bytes 786440 | tf_op jit(solution)/shard_map/ppermute | solution.py:59
  48.0 1.6 %broadcast_in_dim.4 = bf16[8,4,8,4096]{3,2,1,0:T(8,128)(2,1)} broadcast(bf16[4,8,4096]{2,1,0:T(8,128)(2,1)S(1)} %pad_maximum_fusion.3), dimensions={1,2,3} | broadcast | bytes 2359296 | tf_op jit(solution)/shard_map/broadcast_in_dim | solution.py:53
  49.6 14.5 %all-to-all-start = ((bf16[8,4,8,4096]{3,2,1,0:T(8,128)(2,1)}), bf16[8,4,8,4096]{3,2,1,0:T(8,128)(2,1)S(1)}, u32[]{:S(2)}, u32[]{:S(2)}) async-start(bf16[8,4,8,4096]{3,2,1,0:T(8,128)(2,1)} %broadcast_in_dim.4), calls=%async_computation | async-start | bytes 4194304 | tf_op jit(solution)/shard_map/all_to_all | solution.py:53
  64.1 1.7 %collective-permute-done.6 = bf16[2,2,8,4096]{3,2,1,0:T(8,128)(2,1)S(1)} collective-permute-done((bf16[2,2,8,4096]{3,2,1,0:T(8,128)(2,1)S(1)}, bf16[2,2,8,4096]{3,2,1,0:T(8,128)(2,1)S(1)}, u32[]{:S(2)}, u32[]{:S(2)}) %collective-permute-start.6) | collective-permute-done | bytes 262176 | tf_op jit(solution)/shard_map/ppermute | solution.py:59
  65.8 3.2 %collective-permute-start.7 = (bf16[2,4,8,4096]{3,2,1,0:T(8,128)(2,1)S(1)}, bf16[2,4,8,4096]{3,2,1,0:T(8,128)(2,1)S(1)}, u32[]{:S(2)}, u32[]{:S(2)}) collective-permute-start(bf16[2,4,8,4096]{3,2,1,0:T(8,128)(2,1)S(1)} %bitcast.71), channel_id=1, source_target_pairs={{0,2},{2,0},{4,6},{6,4},{8,10},{10,8},{12,14},{14,12},{16,18},{18,... | collective-permute-start | bytes 1572872 | tf_op jit(solution)/shard_map/ppermute | solution.py:59
  69.0 9.7 %collective-permute-done.7 = bf16[2,4,8,4096]{3,2,1,0:T(8,128)(2,1)S(1)} collective-permute-done((bf16[2,4,8,4096]{3,2,1,0:T(8,128)(2,1)S(1)}, bf16[2,4,8,4096]{3,2,1,0:T(8,128)(2,1)S(1)}, u32[]{:S(2)}, u32[]{:S(2)}) %collective-permute-start.7) | collective-permute-done | bytes 524320 | tf_op jit(solution)/shard_map/ppermute | solution.py:59
  78.9 5.2 %collective-permute-start.8 = (bf16[2,8,8,4096]{3,2,1,0:T(8,128)(2,1)S(1)}, bf16[2,8,8,4096]{3,2,1,0:T(8,128)(2,1)}, u32[]{:S(2)}, u32[]{:S(2)}) collective-permute-start(bf16[2,8,8,4096]{3,2,1,0:T(8,128)(2,1)S(1)} %bitcast.66), channel_id=1, source_target_pairs={{0,1},{1,0},{2,3},{3,2},{4,5},{5,4},{6,7},{7,6},{8,9},{9,8},{10,11... | collective-permute-start | bytes 3145736 | tf_op jit(solution)/shard_map/ppermute | solution.py:61
  84.8 4.4 %all-to-all-done = bf16[8,4,8,4096]{3,2,1,0:T(8,128)(2,1)S(1)} async-done(((bf16[8,4,8,4096]{3,2,1,0:T(8,128)(2,1)}), bf16[8,4,8,4096]{3,2,1,0:T(8,128)(2,1)S(1)}, u32[]{:S(2)}, u32[]{:S(2)}) %all-to-all-start) | async-done | bytes 2097184 | tf_op jit(solution)/shard_map/all_to_all | solution.py:53
  90.0 1.7 %multiply_reduce_fusion.1 = f32[2,2,8,8]{3,2,0,1:T(8,128)S(1)} fusion(bf16[2,1,8,8,4096]{4,3,2,0,1:T(8,128)(2,1)} %bitcast.20, bf16[2,1,8,8,4096]{4,3,2,0,1:T(8,128)(2,1)S(1)} %bitcast.67), kind=kLoop, calls=%fused_computation.1 | loop fusion | flops 4194048 | bytes 2098176 | tf_op jit(solution)/shard_map/reduce_sum | solution.py:15
  91.7 2.7 %fusion = (bf16[1,2,8,8,4096]{4,3,2,0,1:T(8,128)(2,1)}, bf16[1,2,8,8,4096]{4,3,2,0,1:T(8,128)(2,1)}) fusion(bf16[2,1,8,8,4096]{4,3,2,0,1:T(8,128)(2,1)S(1)} %bitcast.68, bf16[2,1,8,8,4096]{4,3,2,0,1:T(8,128)(2,1)} %bitcast.20), kind=kLoop, calls=%fused_computation.7 | loop fusion | flops 1048576 | bytes 4194304 | tf_op jit(solution)/shard_map/stack | solution.py:62
  94.5 1.5 %scatter.11 = f32[2,8,128]{2,1,0:T(8,128)S(1)} dynamic-update-slice(f32[2,8,128]{2,1,0:T(8,128)S(1)} %scatter.10, f32[1,2,128]{2,1,0:T(2,128)S(1)} %reshape.153, s32[]{:T(128)} %bitcast.22, s32[]{:T(128)} %bitcast.23, s32[]{:T(128)} %constant.105.clone.1) | dynamic-update-slice | bytes 2052 | tf_op jit(solution)/shard_map/scatter | solution.py:67
  96.1 1.9 %fusion.11 = f32[8,2,16,128]{3,2,1,0:T(8,128)S(1)} fusion(bf16[8,2,16,4096]{3,2,1,0:T(8,128)(2,1)S(1)} %bitcast.64, bf16[128,4096,1,1]{1,0,3,2:T(8,128)(2,1)} %bitcast.70), kind=kOutput, calls=%fused_computation.44 | convolution fusion | flops 268435456 | bytes 3276800 | tf_op jit(solution)/shard_map/dot_general | solution.py:19
  98.1 7.5 %collective-permute-start.9 = (f32[264,128]{1,0:T(8,128)S(1)}, f32[264,128]{1,0:T(8,128)S(1)}, u32[]{:S(2)}, u32[]{:S(2)}) collective-permute-start(f32[264,128]{1,0:T(8,128)S(1)} %pad_maximum_fusion.5), channel_id=1, source_target_pairs={{0,32},{32,0},{1,33},{33,1},{2,34},{34,2},{3,35},{35,3},{4,36},{36... | collective-permute-start | bytes 405512 | tf_op jit(solution)/shard_map/ppermute | solution.py:71
  105.6 0.7 fusion.10
  106.3 1.7 %collective-permute-done.9 = f32[264,128]{1,0:T(8,128)S(1)} collective-permute-done((f32[264,128]{1,0:T(8,128)S(1)}, f32[264,128]{1,0:T(8,128)S(1)}, u32[]{:S(2)}, u32[]{:S(2)}) %collective-permute-start.9) | collective-permute-done | bytes 135200 | tf_op jit(solution)/shard_map/ppermute | solution.py:71
  108.5 0.7 copy.23
  (44 shorter events, 2.3 us)
Async XLA Ops:
  0.9 5.6 %collective-permute-start.4 = (bf16[8,4096]{1,0:T(8,128)(2,1)S(1)}, bf16[8,4096]{1,0:T(8,128)(2,1)S(1)}, u32[]{:S(2)}, u32[]{:S(2)}) collective-permute-start(bf16[8,4096]{1,0:T(8,128)(2,1)S(1)} %get-tuple-element.47), channel_id=1, source_target_pairs={{0,32},{32,0},{1,33},{33,1},{2,34},{34,2},{3,35},{35,3},{4,36},{36... | collective-permute-start | bytes 196616 | tf_op jit(solution)/shard_map/ppermute | solution.py:57
  6.5 39.1 %collective-permute-start.5 = (bf16[2,1,8,4096]{3,2,0,1:T(8,128)(2,1)S(1)}, bf16[2,1,8,4096]{3,2,0,1:T(8,128)(2,1)S(1)}, u32[]{:S(2)}, u32[]{:S(2)}) collective-permute-start(bf16[2,1,8,4096]{3,2,0,1:T(8,128)(2,1)S(1)} %get-tuple-element.50), channel_id=1, source_target_pairs={{0,8},{2,10},{4,12},{6,14},{8,0},{10,2},{12,4},{14,6},{16,24},{18,... | collective-permute-start | bytes 393224 | tf_op jit(solution)/shard_map/ppermute | solution.py:59
  15.6 32.3 %collective-permute-start.3 = (bf16[8,4096]{1,0:T(8,128)(2,1)S(1)}, bf16[8,4096]{1,0:T(8,128)(2,1)S(1)}, u32[]{:S(2)}, u32[]{:S(2)}) collective-permute-start(bf16[8,4096]{1,0:T(8,128)(2,1)S(1)} %get-tuple-element.48), channel_id=1, source_target_pairs={{0,48},{1,32},{2,112},{3,96},{4,176},{5,160},{6,240},{7,224},{8,30... | collective-permute-start | bytes 196616 | tf_op jit(solution)/shard_map/ppermute | solution.py:51
  20.7 27.2 %collective-permute-start.2 = (bf16[8,4096]{1,0:T(8,128)(2,1)S(1)}, bf16[8,4096]{1,0:T(8,128)(2,1)S(1)}, u32[]{:S(2)}, u32[]{:S(2)}) collective-permute-start(bf16[8,4096]{1,0:T(8,128)(2,1)S(1)} %get-tuple-element.48), channel_id=1, source_target_pairs={{0,32},{1,48},{2,96},{3,112},{4,160},{5,176},{6,224},{7,240},{8,28... | collective-permute-start | bytes 196616 | tf_op jit(solution)/shard_map/ppermute | solution.py:51
  31.1 16.9 %collective-permute-start.1 = (bf16[8,4096]{1,0:T(8,128)(2,1)S(1)}, bf16[8,4096]{1,0:T(8,128)(2,1)S(1)}, u32[]{:S(2)}, u32[]{:S(2)}) collective-permute-start(bf16[8,4096]{1,0:T(8,128)(2,1)S(1)} %get-tuple-element.45), channel_id=1, source_target_pairs={{0,16},{1,0},{2,80},{3,64},{4,144},{5,128},{6,208},{7,192},{8,272}... | collective-permute-start | bytes 196616 | tf_op jit(solution)/shard_map/ppermute | solution.py:51
  33.4 14.6 %collective-permute-start = (bf16[8,4096]{1,0:T(8,128)(2,1)S(1)}, bf16[8,4096]{1,0:T(8,128)(2,1)S(1)}, u32[]{:S(2)}, u32[]{:S(2)}) collective-permute-start(bf16[8,4096]{1,0:T(8,128)(2,1)S(1)} %get-tuple-element.45), channel_id=1, source_target_pairs={{0,0},{1,16},{2,64},{3,80},{4,128},{5,144},{6,192},{7,208},{8,256}... | collective-permute-start | bytes 196616 | tf_op jit(solution)/shard_map/ppermute | solution.py:51
  45.7 20.1 %collective-permute-start.6 = (bf16[2,2,8,4096]{3,2,1,0:T(8,128)(2,1)S(1)}, bf16[2,2,8,4096]{3,2,1,0:T(8,128)(2,1)S(1)}, u32[]{:S(2)}, u32[]{:S(2)}) collective-permute-start(bf16[2,2,8,4096]{3,2,1,0:T(8,128)(2,1)S(1)} %get-tuple-element.44), channel_id=1, source_target_pairs={{0,4},{2,6},{4,0},{6,2},{8,12},{10,14},{12,8},{14,10},{16,20},{18,... | collective-permute-start | bytes 786440 | tf_op jit(solution)/shard_map/ppermute | solution.py:59
  49.6 39.6 %all-to-all-start = ((bf16[8,4,8,4096]{3,2,1,0:T(8,128)(2,1)}), bf16[8,4,8,4096]{3,2,1,0:T(8,128)(2,1)S(1)}, u32[]{:S(2)}, u32[]{:S(2)}) async-start(bf16[8,4,8,4096]{3,2,1,0:T(8,128)(2,1)} %broadcast_in_dim.4), calls=%async_computation | async-start | bytes 4194304 | tf_op jit(solution)/shard_map/all_to_all | solution.py:53
  65.8 12.9 %collective-permute-start.7 = (bf16[2,4,8,4096]{3,2,1,0:T(8,128)(2,1)S(1)}, bf16[2,4,8,4096]{3,2,1,0:T(8,128)(2,1)S(1)}, u32[]{:S(2)}, u32[]{:S(2)}) collective-permute-start(bf16[2,4,8,4096]{3,2,1,0:T(8,128)(2,1)S(1)} %bitcast.71), channel_id=1, source_target_pairs={{0,2},{2,0},{4,6},{6,4},{8,10},{10,8},{12,14},{14,12},{16,18},{18,... | collective-permute-start | bytes 1572872 | tf_op jit(solution)/shard_map/ppermute | solution.py:59
  78.9 11.0 %collective-permute-start.8 = (bf16[2,8,8,4096]{3,2,1,0:T(8,128)(2,1)S(1)}, bf16[2,8,8,4096]{3,2,1,0:T(8,128)(2,1)}, u32[]{:S(2)}, u32[]{:S(2)}) collective-permute-start(bf16[2,8,8,4096]{3,2,1,0:T(8,128)(2,1)S(1)} %bitcast.66), channel_id=1, source_target_pairs={{0,1},{1,0},{2,3},{3,2},{4,5},{5,4},{6,7},{7,6},{8,9},{9,8},{10,11... | collective-permute-start | bytes 3145736 | tf_op jit(solution)/shard_map/ppermute | solution.py:61
  94.4 11.2 %copy-start = (bf16[1,2,8,8,4096]{4,3,2,0,1:T(8,128)(2,1)S(1)}, bf16[1,2,8,8,4096]{4,3,2,0,1:T(8,128)(2,1)}, u32[]{:S(2)}) copy-start(bf16[1,2,8,8,4096]{4,3,2,0,1:T(8,128)(2,1)} %get-tuple-element.41) | copy-start | bytes 3145732
  98.1 9.9 %collective-permute-start.9 = (f32[264,128]{1,0:T(8,128)S(1)}, f32[264,128]{1,0:T(8,128)S(1)}, u32[]{:S(2)}, u32[]{:S(2)}) collective-permute-start(f32[264,128]{1,0:T(8,128)S(1)} %pad_maximum_fusion.5), channel_id=1, source_target_pairs={{0,32},{32,0},{1,33},{33,1},{2,34},{34,2},{3,35},{35,3},{4,36},{36... | collective-permute-start | bytes 405512 | tf_op jit(solution)/shard_map/ppermute | solution.py:71

commit v6 on v3

--- a/solution.py
+++ b/solution.py
@@ -37,15 +37,19 @@
 
     columns = lax.all_to_all(jnp.concatenate([held, held]), ("zh", "za"), 0, 0)
     columns = to_all(columns, "x", 4).reshape(2, 2, 16, count, part)
-    columns = lax.all_to_all(columns.swapaxes(0, 1), "core", 0, 0)
-    columns = columns.transpose(1, 2, 0, 3, 4).reshape(2, 32 * count, part)
+    core = lax.axis_index("core")
+    keep = jnp.where(core == 0, columns[:, 0], columns[:, 1])
+    give = jnp.where(core == 0, columns[:, 1], columns[:, 0])
+    give = lax.ppermute(give, "core", [(0, 1), (1, 0)])
+    columns = jnp.where(core == 0, jnp.stack([keep, give], 2), jnp.stack([give, keep], 2))
+    columns = columns.reshape(2, 32 * count, part)
 
     rows = held[:, None]
     for step in (2, 1):
         other = lax.ppermute(rows, "za", [(z, z ^ step) for z in range(4)])
         rows = jnp.stack([rows, other], axis=2).reshape(4, -1, 2 * count, part)
-    rows = to_all(rows, "core", 2)
-    rows = rows.swapaxes(0, 1).reshape(4, 16 * count, part)
+    other = lax.ppermute(rows, "core", [(0, 1), (1, 0)])
+    rows = jnp.stack([rows, other], axis=1).reshape(4, 16 * count, part)
 
     products = cross(rows.reshape(64 * count, part), columns.reshape(64 * count, part))
     products = products.reshape(4, 16 * count, 2, 32 * count).swapaxes(1, 2)
@@ -59,6 +63,7 @@
     gram = left[:, None] * total[: 16 * count] * right[None, :]
 
     gram = gram.reshape(2, 2, 2, 2, count, 32 * count)
+    gram = swap(lax.axis_index("core"), gram, 0)
     gram = swap(za >> 1, gram, 1)
     gram = swap(za & 1, gram, 2)
     return gram.transpose(1, 2, 3, 0, 4, 5).reshape(16 * count, 32 * count)

time: 132 us -> 101 us (0.77)
  blocking collectives: 64.1 us -> 11.9 us
  starting transfers between devices: 24.7 us -> 38.3 us
  waiting for transfers between devices: 37.4 us -> 42.5 us
  other arithmetic: 2.61 us -> 5.71 us
    all_to_all x3 -> x0, blocking collectives: 52.2 us -> none  [the longest x1 32.1 us: body(): columns = lax.all_to_all(jnp.concatenate([held, held]), ('zh', 'za'), 0, 0)]
    all_to_all x0 -> x1, starting transfers between devices: none -> 13.9 us  [body(): columns = lax.all_to_all(jnp.concatenate([held, held]), ('zh', 'za'), 0, 0)]
    all_to_all x1, waiting for transfers between devices: 13.8 us -> 0.01 us  [to_all(): lax.all_to_all(jnp.broadcast_to(array[None], (size, *array.shape)), axes,...]
    all_to_all x0 -> x1, waiting for transfers between devices: none -> 10.3 us  [body(): columns = lax.all_to_all(jnp.concatenate([held, held]), ('zh', 'za'), 0, 0)]
    ppermute x2, starting transfers between devices: 17.2 us -> 9.19 us  [body(): other = lax.ppermute(rows, 'za', [(z, z ^ step) for z in range(4)])]
    ppermute x0 -> x2, starting transfers between devices: none -> 7.6 us  [the longest x1 5.7 us: body(): other = lax.ppermute(rows, 'core', [(0, 1), (1, 0)])]
    ppermute x2, waiting for transfers between devices: 7.48 us -> 14.2 us  [body(): other = lax.ppermute(rows, 'za', [(z, z ^ step) for z in range(4)])]
    ppermute x0 -> x2, waiting for transfers between devices: none -> 1.64 us  [the longest x1 1.64 us: body(): give = lax.ppermute(give, 'core', [(0, 1), (1, 0)])]
  transfers between devices with their start and end apart: 4 -> 7, of which waited for: 4 -> 5; matrix products, arithmetic and copies ran while one was open for 0% -> 3% of each run, Pallas kernels for 0% -> 0%
where the time goes in v6:
time: 101 us
  waiting for transfers between devices  42.5 us (42%)
  starting transfers between devices  38.3 us (38%)
  blocking collectives  11.9 us (12%)
  other arithmetic  5.71 us (6%)
  local copies, waits for them, and re-layouts  1.5 us (1%)
    all_to_all x1, waiting for transfers between devices, body(): total = jnp.sum(lax.all_to_all(message, SUM, 0, 0), axis=0)  16.4 us
    ppermute x2, waiting for transfers between devices, body(): other = lax.ppermute(rows, 'za', [(z, z ^ step) for z in range(4)])  14.2 us
    all_to_all x1, starting transfers between devices, body(): columns = lax.all_to_all(jnp.concatenate([held, held]), ('zh', 'za'), 0, 0)  13.9 us
    all_to_all x1, blocking collectives, body(): lax.all_to_all(grads.reshape(count, 8, part).transpose(1, 0, 2), SUM, 0, 0)  11.9 us
    all_to_all x1, waiting for transfers between devices, body(): columns = lax.all_to_all(jnp.concatenate([held, held]), ('zh', 'za'), 0, 0)  10.3 us
    ppermute x2, starting transfers between devices, body(): other = lax.ppermute(rows, 'za', [(z, z ^ step) for z in range(4)])  9.19 us
    ppermute x1, starting transfers between devices, body(): other = lax.ppermute(rows, 'core', [(0, 1), (1, 0)])  5.7 us
    all_to_all x1, starting transfers between devices, to_all(): lax.all_to_all(jnp.broadcast_to(array[None], (size, *array.shape)), axes,...  4.01 us
  transfers between devices with their start and end apart: 7, of which 5 were waited for; matrix products, arithmetic and copies ran while one was open for 3% of the time, Pallas kernels for 0%

profile of v6, /device:TPU:1, one launch (start us, length us, event | category | flops | bytes accessed | tf_op | source)
XLA Modules:
  0.0 100.9 jit_solution(15610290485511485154)
XLA Ops:
  0.0 11.9 %all_to_all.20 = bf16[8,8,1024]{2,1,0:T(8,128)(2,1)S(1)} all-to-all(bf16[8,8,1024]{2,1,0:T(8,128)(2,1)} %bitcast.71), channel_id=1, replica_groups=mesh['y'=4,'x'=4,'zh'=2,'za'=4,'zb'=2,'core'=2] {'y','zb'}, dimensions={0} | all-to-all | bytes 262144 | tf_op jit(solution)/shard_map/all_to_all | solution.py:35
  11.9 0.7 pad_maximum_fusion.4
  12.6 13.9 %all-to-all-start.1 = ((bf16[8,16,1024]{2,1,0:T(8,128)(2,1)}), bf16[8,16,1024]{2,1,0:T(8,128)(2,1)S(1)}, u32[]{:S(2)}, u32[]{:S(2)}) async-start(bf16[8,16,1024]{2,1,0:T(8,128)(2,1)} %pad_maximum_fusion.4), calls=%async_computation.1 | async-start | bytes 524288 | tf_op jit(solution)/shard_map/all_to_all | solution.py:38
  26.6 7.3 %collective-permute-start = (bf16[4,1,16,1024]{3,2,0,1:T(8,128)(2,1)S(1)}, bf16[4,1,16,1024]{3,2,0,1:T(8,128)(2,1)S(1)}, u32[]{:S(2)}, u32[]{:S(2)}) collective-permute-start(bf16[4,1,16,1024]{3,2,0,1:T(8,128)(2,1)S(1)} %bitcast.65), channel_id=1, source_target_pairs={{0,8},{4,12},{8,0},{12,4},{1,9},{5,13},{9,1},{13,5},{2,10},{6,14},... | collective-permute-start | bytes 393224 | tf_op jit(solution)/shard_map/ppermute | solution.py:49
  33.8 10.3 %all-to-all-done.1 = bf16[8,16,1024]{2,1,0:T(8,128)(2,1)S(1)} async-done(((bf16[8,16,1024]{2,1,0:T(8,128)(2,1)}), bf16[8,16,1024]{2,1,0:T(8,128)(2,1)S(1)}, u32[]{:S(2)}, u32[]{:S(2)}) %all-to-all-start.1) | async-done | bytes 262176 | tf_op jit(solution)/shard_map/all_to_all | solution.py:38
  44.1 1.1 %broadcast_in_dim.6 = bf16[4,8,16,1024]{3,2,1,0:T(8,128)(2,1)} broadcast(bf16[8,16,1024]{2,1,0:T(8,128)(2,1)S(1)} %all-to-all-done.1), dimensions={1,2,3} | broadcast | bytes 1310720 | tf_op jit(solution)/shard_map/broadcast_in_dim | solution.py:27
  45.2 4.0 %all-to-all-start.2 = ((bf16[4,8,16,1024]{3,2,1,0:T(8,128)(2,1)}), bf16[4,8,16,1024]{3,2,1,0:T(8,128)(2,1)S(1)}, u32[]{:S(2)}, u32[]{:S(2)}) async-start(bf16[4,8,16,1024]{3,2,1,0:T(8,128)(2,1)} %broadcast_in_dim.6), calls=%async_computation.2 | async-start | bytes 2097152 | tf_op jit(solution)/shard_map/all_to_all | solution.py:27
  49.2 5.9 %collective-permute-done = bf16[4,1,16,1024]{3,2,0,1:T(8,128)(2,1)S(1)} collective-permute-done((bf16[4,1,16,1024]{3,2,0,1:T(8,128)(2,1)S(1)}, bf16[4,1,16,1024]{3,2,0,1:T(8,128)(2,1)S(1)}, u32[]{:S(2)}, u32[]{:S(2)}) %collective-permute-start) | collective-permute-done | bytes 131104 | tf_op jit(solution)/shard_map/ppermute | solution.py:49
  55.2 1.9 %collective-permute-start.1 = (bf16[4,2,16,1024]{3,2,1,0:T(8,128)(2,1)S(1)}, bf16[4,2,16,1024]{3,2,1,0:T(8,128)(2,1)S(1)}, u32[]{:S(2)}, u32[]{:S(2)}) collective-permute-start(bf16[4,2,16,1024]{3,2,1,0:T(8,128)(2,1)S(1)} %get-tuple-element.32), channel_id=1, source_target_pairs={{0,4},{4,0},{8,12},{12,8},{1,5},{5,1},{9,13},{13,9},{2,6},{6,2},{1... | collective-permute-start | bytes 786440 | tf_op jit(solution)/shard_map/ppermute | solution.py:49
  57.1 8.3 %collective-permute-done.1 = bf16[4,2,16,1024]{3,2,1,0:T(8,128)(2,1)S(1)} collective-permute-done((bf16[4,2,16,1024]{3,2,1,0:T(8,128)(2,1)S(1)}, bf16[4,2,16,1024]{3,2,1,0:T(8,128)(2,1)S(1)}, u32[]{:S(2)}, u32[]{:S(2)}) %collective-permute-start.1) | collective-permute-done | bytes 262176 | tf_op jit(solution)/shard_map/ppermute | solution.py:49
  65.5 5.7 %collective-permute-start.2 = (bf16[4,4,16,1024]{3,2,1,0:T(8,128)(2,1)S(1)}, bf16[4,4,16,1024]{3,2,1,0:T(8,128)(2,1)S(1)}, u32[]{:S(2)}, u32[]{:S(2)}) collective-permute-start(bf16[4,4,16,1024]{3,2,1,0:T(8,128)(2,1)S(1)} %bitcast.59), channel_id=1, source_target_pairs={{0,1},{1,0},{2,3},{3,2},{4,5},{5,4},{6,7},{7,6},{8,9},{9,8},{10,11... | collective-permute-start | bytes 1572872 | tf_op jit(solution)/shard_map/ppermute | solution.py:51
  71.2 0.8 fusion
  72.1 1.9 %collective-permute-start.3 = (bf16[2,16,8,1024]{3,2,1,0:T(8,128)(2,1)}, bf16[2,16,8,1024]{3,2,1,0:T(8,128)(2,1)}, u32[]{:S(2)}, u32[]{:S(2)}) collective-permute-start(bf16[2,16,8,1024]{3,2,1,0:T(8,128)(2,1)} %fusion), channel_id=1, source_target_pairs={{0,1},{1,0},{2,3},{3,2},{4,5},{5,4},{6,7},{7,6},{8,9},{9,8},{10,11... | collective-permute-start | bytes 1572872 | tf_op jit(solution)/shard_map/ppermute | solution.py:43
  74.0 0.3 multiply_reduce_fusion.1
  74.3 0.1 broadcast_in_dim.7
  74.4 0.1 pad_maximum_fusion.1
  74.6 1.6 %collective-permute-done.3 = bf16[2,16,8,1024]{3,2,1,0:T(8,128)(2,1)} collective-permute-done((bf16[2,16,8,1024]{3,2,1,0:T(8,128)(2,1)}, bf16[2,16,8,1024]{3,2,1,0:T(8,128)(2,1)}, u32[]{:S(2)}, u32[]{:S(2)}) %collective-permute-start.3) | collective-permute-done | bytes 524320 | tf_op jit(solution)/shard_map/ppermute | solution.py:43
  76.2 1.7 %multiply_reduce_fusion = (f32[2,16,2,8]{3,1,0,2:T(8,128)S(1)}, bf16[2,16,2,8,1024]{4,3,1,0,2:T(8,128)(2,1)S(1)}) fusion(bf16[2,16,1,8,1024]{4,3,1,0,2:T(8,128)(2,1)S(1)} %fusion.1, bf16[2,16,1,8,1024]{4,3,1,0,2:T(8,128)(2,1)} %bitcast.23, pred[]{:T(512)S(6)} %eq.17), kind=kLoop, calls=%fused_computation | loop fusion | flops 3145216 | bytes 2099201 | tf_op jit(solution)/shard_map/reduce_sum | solution.py:13
  77.9 0.1 broadcast_in_dim.8
  78.1 0.7 convolution_bitcast_fusion
  78.9 1.1 %pad_maximum_fusion = f32[4,2,136,256]{3,2,1,0:T(8,128)} fusion(f32[4,2,8,256]{3,2,1,0:T(8,128)S(1)} %scatter.9, f32[4,2,128,256]{3,2,1,0:T(8,128)S(1)} %convolution_bitcast_fusion), kind=kLoop, calls=%fused_computation.3 | loop fusion | flops 278528 | bytes 2228224 | tf_op jit(solution)/shard_map/concatenate | solution.py:59
  80.0 3.6 %all-to-all-start.3 = ((f32[8,136,256]{2,1,0:T(8,128)}), f32[8,136,256]{2,1,0:T(8,128)S(1)}, u32[]{:S(2)}, u32[]{:S(2)}) async-start(f32[8,136,256]{2,1,0:T(8,128)} %bitcast.27), calls=%async_computation.3 | async-start | bytes 2228224 | tf_op jit(solution)/shard_map/all_to_all | solution.py:60
  83.6 16.4 %all-to-all-done.3 = f32[8,136,256]{2,1,0:T(8,128)S(1)} async-done(((f32[8,136,256]{2,1,0:T(8,128)}), f32[8,136,256]{2,1,0:T(8,128)S(1)}, u32[]{:S(2)}, u32[]{:S(2)}) %all-to-all-start.3) | async-done | bytes 1114144 | tf_op jit(solution)/shard_map/all_to_all | solution.py:60
  100.2 0.7 reverse_select_fusion
  (18 shorter events, 0.6 us)
Async XLA Ops:
  12.6 31.5 %all-to-all-start.1 = ((bf16[8,16,1024]{2,1,0:T(8,128)(2,1)}), bf16[8,16,1024]{2,1,0:T(8,128)(2,1)S(1)}, u32[]{:S(2)}, u32[]{:S(2)}) async-start(bf16[8,16,1024]{2,1,0:T(8,128)(2,1)} %pad_maximum_fusion.4), calls=%async_computation.1 | async-start | bytes 524288 | tf_op jit(solution)/shard_map/all_to_all | solution.py:38
  26.6 28.6 %collective-permute-start = (bf16[4,1,16,1024]{3,2,0,1:T(8,128)(2,1)S(1)}, bf16[4,1,16,1024]{3,2,0,1:T(8,128)(2,1)S(1)}, u32[]{:S(2)}, u32[]{:S(2)}) collective-permute-start(bf16[4,1,16,1024]{3,2,0,1:T(8,128)(2,1)S(1)} %bitcast.65), channel_id=1, source_target_pairs={{0,8},{4,12},{8,0},{12,4},{1,9},{5,13},{9,1},{13,5},{2,10},{6,14},... | collective-permute-start | bytes 393224 | tf_op jit(solution)/shard_map/ppermute | solution.py:49
  45.2 26.0 %all-to-all-start.2 = ((bf16[4,8,16,1024]{3,2,1,0:T(8,128)(2,1)}), bf16[4,8,16,1024]{3,2,1,0:T(8,128)(2,1)S(1)}, u32[]{:S(2)}, u32[]{:S(2)}) async-start(bf16[4,8,16,1024]{3,2,1,0:T(8,128)(2,1)} %broadcast_in_dim.6), calls=%async_computation.2 | async-start | bytes 2097152 | tf_op jit(solution)/shard_map/all_to_all | solution.py:27
  55.2 10.3 %collective-permute-start.1 = (bf16[4,2,16,1024]{3,2,1,0:T(8,128)(2,1)S(1)}, bf16[4,2,16,1024]{3,2,1,0:T(8,128)(2,1)S(1)}, u32[]{:S(2)}, u32[]{:S(2)}) collective-permute-start(bf16[4,2,16,1024]{3,2,1,0:T(8,128)(2,1)S(1)} %get-tuple-element.32), channel_id=1, source_target_pairs={{0,4},{4,0},{8,12},{12,8},{1,5},{5,1},{9,13},{13,9},{2,6},{6,2},{1... | collective-permute-start | bytes 786440 | tf_op jit(solution)/shard_map/ppermute | solution.py:49
  65.5 8.5 %collective-permute-start.2 = (bf16[4,4,16,1024]{3,2,1,0:T(8,128)(2,1)S(1)}, bf16[4,4,16,1024]{3,2,1,0:T(8,128)(2,1)S(1)}, u32[]{:S(2)}, u32[]{:S(2)}) collective-permute-start(bf16[4,4,16,1024]{3,2,1,0:T(8,128)(2,1)S(1)} %bitcast.59), channel_id=1, source_target_pairs={{0,1},{1,0},{2,3},{3,2},{4,5},{5,4},{6,7},{7,6},{8,9},{9,8},{10,11... | collective-permute-start | bytes 1572872 | tf_op jit(solution)/shard_map/ppermute | solution.py:51
  72.1 4.1 %collective-permute-start.3 = (bf16[2,16,8,1024]{3,2,1,0:T(8,128)(2,1)}, bf16[2,16,8,1024]{3,2,1,0:T(8,128)(2,1)}, u32[]{:S(2)}, u32[]{:S(2)}) collective-permute-start(bf16[2,16,8,1024]{3,2,1,0:T(8,128)(2,1)} %fusion), channel_id=1, source_target_pairs={{0,1},{1,0},{2,3},{3,2},{4,5},{5,4},{6,7},{7,6},{8,9},{9,8},{10,11... | collective-permute-start | bytes 1572872 | tf_op jit(solution)/shard_map/ppermute | solution.py:43
  80.0 19.9 %all-to-all-start.3 = ((f32[8,136,256]{2,1,0:T(8,128)}), f32[8,136,256]{2,1,0:T(8,128)S(1)}, u32[]{:S(2)}, u32[]{:S(2)}) async-start(f32[8,136,256]{2,1,0:T(8,128)} %bitcast.27), calls=%async_computation.3 | async-start | bytes 2228224 | tf_op jit(solution)/shard_map/all_to_all | solution.py:60

commit v7 on v3

v7 whole, which is shorter than its diff:
```python
import jax
import jax.numpy as jnp
from jax import lax
from jax.sharding import Mesh, PartitionSpec as P

AXES = ("y", "xh", "xl", "zh", "za", "zb", "core")
SIZES = (4, 2, 2, 2, 4, 2, 2)
SUM = ("y", "zb")
TRADE = [(0, 1), (1, 0)]


def squares(block):
    wide = block.astype(jnp.float32)
    return jnp.sum(wide * wide, axis=-1)


def cross(left, right):
    return lax.dot_general(
        left, right, (((1,), (1,)), ((), ())), preferred_element_type=jnp.float32
    )


def swap(flag, array, axis):
    return jnp.where(flag == 1, jnp.flip(array, axis), array)


def body(grads):
    count, depth = grads.shape
    part = depth // 8
    za, core = (lax.axis_index(a) for a in ("za", "core"))

    held = lax.all_to_all(grads.reshape(count, 8, part).transpose(1, 0, 2), SUM, 0, 0)
    held = held.reshape(4, 2 * count, part)

    columns = lax.all_to_all(jnp.concatenate([held, held]), ("zh", "za"), 0, 0)
    columns = columns.reshape(16 * count, part)
    columns = lax.all_to_all(jnp.broadcast_to(columns[None], (4, *columns.shape)), ("xh", "xl"), 0, 0)
    columns = columns.reshape(2, 2, 16 * count, part)
    own = lax.dynamic_index_in_dim(columns, core, 1, keepdims=False)
    other = lax.ppermute(lax.dynamic_index_in_dim(columns, 1 - core, 1, keepdims=False), "core", TRADE)
    blocks = [block.reshape(32 * count, part) for block in (own, other)]

    rows = held[:, None]
    for step in (2, 1):
        other = lax.ppermute(rows, "za", [(z, z ^ step) for z in range(4)])
        rows = jnp.stack([rows, other], axis=2).reshape(4, -1, 2 * count, part)
    other = lax.ppermute(rows, "core", TRADE)
    rows = jnp.stack([rows, other], axis=1).reshape(4, 16 * count, part)

    lines = rows.reshape(64 * count, part)
    products = jnp.stack([cross(block, lines).reshape(2, 16 * count, 4, -1) for block in blocks], axis=1)
    products = products.reshape(2, 32 * count, 4, -1).transpose(2, 0, 1, 3)
    wide = jnp.stack([squares(block).reshape(2, -1) for block in blocks], axis=1)
    extra = jnp.zeros((4, 2, 8, 16 * count), jnp.float32)
    extra = extra.at[:, :, 0].set(squares(rows)[:, None])
    extra = extra.at[:, :, 1:3].set(wide[None])
    message = jnp.concatenate([products, extra], axis=2)
    total = jnp.sum(lax.all_to_all(message.reshape(8, -1, 16 * count), SUM, 0, 0), axis=0)
    gram, extra = total[: 32 * count], lax.rsqrt(total[32 * count :] + 1e-06)
    gram = gram * extra[1:3].reshape(-1)[:, None] * extra[0]

    gram = swap(core, gram.reshape(2, 16, count, -1), 0).swapaxes(0, 1)
    gram = gram.reshape(32 * count, -1).T.reshape(2, 2, 2, 2, count, -1)
    for axis, flag in ((0, core), (1, za >> 1), (2, za & 1)):
        gram = swap(flag, gram, axis)
    return gram.transpose(1, 2, 3, 0, 4, 5).reshape(16 * count, -1)


def solution(mesh):
    fine = Mesh(mesh.devices.reshape(SIZES), AXES)
    return jax.shard_map(
        body,
        mesh=fine,
        in_specs=(P(AXES, None),),
        out_specs=P(("y", "xh", "xl", "zh"), ("za", "zb", "core")),
        check_vma=False,
    )
```

time: 132 us -> 98.4 us (0.75)
  blocking collectives: 64.1 us -> 11.9 us
  starting transfers between devices: 24.7 us -> 38.3 us
  waiting for transfers between devices: 37.4 us -> 41.2 us
  local copies, waits for them, and re-layouts: 1.82 us -> 3.32 us
    all_to_all x3 -> x0, blocking collectives: 52.2 us -> none  [the longest x1 32.1 us: body(): columns = lax.all_to_all(jnp.concatenate([held, held]), ('zh', 'za'), 0, 0)]
    all_to_all x2 -> x3, starting transfers between devices: 7.57 us -> 21.5 us  [the longest x1 13.9 us: body(): columns = lax.all_to_all(jnp.concatenate([held, held]), ('zh', 'za'), 0, 0)]
    ppermute x2, starting transfers between devices: 17.2 us -> 9.19 us  [body(): other = lax.ppermute(rows, 'za', [(z, z ^ step) for z in range(4)])]
    ppermute x0 -> x2, starting transfers between devices: none -> 7.64 us  [the longest x1 5.72 us: body(): other = lax.ppermute(rows, 'core', TRADE)]
    ppermute x2, waiting for transfers between devices: 7.48 us -> 14.2 us  [body(): other = lax.ppermute(rows, 'za', [(z, z ^ step) for z in range(4)])]
    all_to_all x2 -> x3, waiting for transfers between devices: 29.9 us -> 26.3 us  [the longest x1 16 us: body(): lax.all_to_all(message.reshape(8, -1, 16 * count), SUM, 0, 0)]
  transfers between devices with their start and end apart: 4 -> 7, of which waited for: 4 -> 5; matrix products, arithmetic and copies ran while one was open for 0% -> 2% of each run, Pallas kernels for 0% -> 0%
where the time goes in v7:
time: 98.4 us; the launch traced here: 97.9 us
  waiting for transfers between devices  41.2 us (42%)
  starting transfers between devices  38.3 us (39%)
  blocking collectives  11.9 us (12%)
  local copies, waits for them, and re-layouts  3.32 us (3%)
  other arithmetic  1.93 us (2%)
    all_to_all x1, waiting for transfers between devices, body(): lax.all_to_all(message.reshape(8, -1, 16 * count), SUM, 0, 0)  16 us
    ppermute x2, waiting for transfers between devices, body(): other = lax.ppermute(rows, 'za', [(z, z ^ step) for z in range(4)])  14.2 us
    all_to_all x1, starting transfers between devices, body(): columns = lax.all_to_all(jnp.concatenate([held, held]), ('zh', 'za'), 0, 0)  13.9 us
    all_to_all x1, blocking collectives, body(): lax.all_to_all(grads.reshape(count, 8, part).transpose(1, 0, 2), SUM, 0, 0)  11.9 us
    all_to_all x1, waiting for transfers between devices, body(): columns = lax.all_to_all(jnp.concatenate([held, held]), ('zh', 'za'), 0, 0)  10.3 us
    ppermute x2, starting transfers between devices, body(): other = lax.ppermute(rows, 'za', [(z, z ^ step) for z in range(4)])  9.19 us
    ppermute x1, starting transfers between devices, body(): other = lax.ppermute(rows, 'core', TRADE)  5.72 us
    all_to_all x1, starting transfers between devices, body(): lax.all_to_all(jnp.broadcast_to(columns[None], (4, *columns.shape)), ('xh...  4.01 us
  transfers between devices with their start and end apart: 7, of which 5 were waited for; matrix products, arithmetic and copies ran while one was open for 2% of the time, Pallas kernels for 0%

profile of v7, /device:TPU:1, one launch (start us, length us, event | category | flops | bytes accessed | tf_op | source)
XLA Modules:
  0.0 97.9 jit_solution(15383676193596522548)
XLA Ops:
  0.0 11.9 %all_to_all.20 = bf16[8,8,1024]{2,1,0:T(8,128)(2,1)S(1)} all-to-all(bf16[8,8,1024]{2,1,0:T(8,128)(2,1)} %bitcast.82), channel_id=1, replica_groups=mesh['y'=4,'xh'=2,'xl'=2,'zh'=2,'za'=4,'zb'=2,'core'=2] {'y','zb'}, dimensions={0} | all-to-all | bytes 262144 | tf_op jit(solution)/shard_map/all_to_all | solution.py:32
  11.9 0.7 pad_maximum_fusion.4
  12.6 13.9 %all-to-all-start.1 = ((bf16[8,16,1024]{2,1,0:T(8,128)(2,1)}), bf16[8,16,1024]{2,1,0:T(8,128)(2,1)S(1)}, u32[]{:S(2)}, u32[]{:S(2)}) async-start(bf16[8,16,1024]{2,1,0:T(8,128)(2,1)} %pad_maximum_fusion.4), calls=%async_computation.1 | async-start | bytes 524288 | tf_op jit(solution)/shard_map/all_to_all | solution.py:35
  26.6 7.3 %collective-permute-start = (bf16[4,1,16,1024]{3,2,0,1:T(8,128)(2,1)S(1)}, bf16[4,1,16,1024]{3,2,0,1:T(8,128)(2,1)S(1)}, u32[]{:S(2)}, u32[]{:S(2)}) collective-permute-start(bf16[4,1,16,1024]{3,2,0,1:T(8,128)(2,1)S(1)} %bitcast.75), channel_id=1, source_target_pairs={{0,8},{4,12},{8,0},{12,4},{1,9},{5,13},{9,1},{13,5},{2,10},{6,14},... | collective-permute-start | bytes 393224 | tf_op jit(solution)/shard_map/ppermute | solution.py:45
  33.8 10.3 %all-to-all-done.1 = bf16[8,16,1024]{2,1,0:T(8,128)(2,1)S(1)} async-done(((bf16[8,16,1024]{2,1,0:T(8,128)(2,1)}), bf16[8,16,1024]{2,1,0:T(8,128)(2,1)S(1)}, u32[]{:S(2)}, u32[]{:S(2)}) %all-to-all-start.1) | async-done | bytes 262176 | tf_op jit(solution)/shard_map/all_to_all | solution.py:35
  44.1 1.1 %broadcast_in_dim.7 = bf16[4,128,1024]{2,1,0:T(8,128)(2,1)} broadcast(bf16[128,1024]{1,0:T(8,128)(2,1)S(1)} %bitcast.77), dimensions={1,2} | broadcast | bytes 1310720 | tf_op jit(solution)/shard_map/broadcast_in_dim | solution.py:37
  45.3 4.0 %all-to-all-start.2 = ((bf16[4,128,1024]{2,1,0:T(8,128)(2,1)}), bf16[4,128,1024]{2,1,0:T(8,128)(2,1)S(1)}, u32[]{:S(2)}, u32[]{:S(2)}) async-start(bf16[4,128,1024]{2,1,0:T(8,128)(2,1)} %broadcast_in_dim.7), calls=%async_computation.2 | async-start | bytes 2097152 | tf_op jit(solution)/shard_map/all_to_all | solution.py:37
  49.3 5.9 %collective-permute-done = bf16[4,1,16,1024]{3,2,0,1:T(8,128)(2,1)S(1)} collective-permute-done((bf16[4,1,16,1024]{3,2,0,1:T(8,128)(2,1)S(1)}, bf16[4,1,16,1024]{3,2,0,1:T(8,128)(2,1)S(1)}, u32[]{:S(2)}, u32[]{:S(2)}) %collective-permute-start) | collective-permute-done | bytes 131104 | tf_op jit(solution)/shard_map/ppermute | solution.py:45
  55.2 1.9 %collective-permute-start.1 = (bf16[4,2,16,1024]{3,2,1,0:T(8,128)(2,1)S(1)}, bf16[4,2,16,1024]{3,2,1,0:T(8,128)(2,1)S(1)}, u32[]{:S(2)}, u32[]{:S(2)}) collective-permute-start(bf16[4,2,16,1024]{3,2,1,0:T(8,128)(2,1)S(1)} %get-tuple-element.30), channel_id=1, source_target_pairs={{0,4},{4,0},{8,12},{12,8},{1,5},{5,1},{9,13},{13,9},{2,6},{6,2},{1... | collective-permute-start | bytes 786440 | tf_op jit(solution)/shard_map/ppermute | solution.py:45
  57.1 8.3 %collective-permute-done.1 = bf16[4,2,16,1024]{3,2,1,0:T(8,128)(2,1)S(1)} collective-permute-done((bf16[4,2,16,1024]{3,2,1,0:T(8,128)(2,1)S(1)}, bf16[4,2,16,1024]{3,2,1,0:T(8,128)(2,1)S(1)}, u32[]{:S(2)}, u32[]{:S(2)}) %collective-permute-start.1) | collective-permute-done | bytes 262176 | tf_op jit(solution)/shard_map/ppermute | solution.py:45
  65.5 5.7 %collective-permute-start.2 = (bf16[4,4,16,1024]{3,2,1,0:T(8,128)(2,1)S(1)}, bf16[4,4,16,1024]{3,2,1,0:T(8,128)(2,1)S(1)}, u32[]{:S(2)}, u32[]{:S(2)}) collective-permute-start(bf16[4,4,16,1024]{3,2,1,0:T(8,128)(2,1)S(1)} %bitcast.68), channel_id=1, source_target_pairs={{0,1},{1,0},{2,3},{3,2},{4,5},{5,4},{6,7},{7,6},{8,9},{9,8},{10,11... | collective-permute-start | bytes 1572872 | tf_op jit(solution)/shard_map/ppermute | solution.py:47
  71.3 1.9 %collective-permute-start.3 = (bf16[2,128,1024]{2,1,0:T(8,128)(2,1)S(1)}, bf16[2,128,1024]{2,1,0:T(8,128)(2,1)S(1)}, u32[]{:S(2)}, u32[]{:S(2)}) collective-permute-start(bf16[2,128,1024]{2,1,0:T(8,128)(2,1)S(1)} %dynamic-slice_bitcast_fusion), channel_id=1, source_target_pairs={{0,1},{1,0},{2,3},{3,2},{4,5},{5,4},{6,7},{7,6},{8,9},{9,8},{10,11... | collective-permute-start | bytes 1572872 | tf_op jit(solution)/shard_map/ppermute | solution.py:40
  73.2 0.3 multiply_reduce_fusion
  73.6 0.1 pad_maximum_fusion.1
  73.7 0.2 multiply_reduce_fusion.2
  73.9 0.5 convolution_bitcast_fusion.1
  74.4 0.7 collective-permute-done.3
  75.1 0.5 convolution_bitcast_fusion
  75.7 0.2 multiply_reduce_fusion.1
  76.0 0.1 scatter.9
  76.2 1.1 %copy.12 = f32[4,2,264,128]{3,2,1,0:T(8,128)} copy(f32[4,2,264,128]{3,2,0,1:T(8,128)S(1)} %pad_maximum_fusion) | data formatting | bytes 2162688 | tf_op jit(solution)/shard_map/concatenate | solution.py:57
  77.2 3.6 %all-to-all-start.3 = ((f32[8,264,128]{2,1,0:T(8,128)}), f32[8,264,128]{2,1,0:T(8,128)S(1)}, u32[]{:S(2)}, u32[]{:S(2)}) async-start(f32[8,264,128]{2,1,0:T(8,128)} %bitcast.31), calls=%async_computation.3 | async-start | bytes 2162688 | tf_op jit(solution)/shard_map/all_to_all | solution.py:58
  80.8 16.0 %all-to-all-done.3 = f32[8,264,128]{2,1,0:T(8,128)S(1)} async-done(((f32[8,264,128]{2,1,0:T(8,128)}), f32[8,264,128]{2,1,0:T(8,128)S(1)}, u32[]{:S(2)}, u32[]{:S(2)}) %all-to-all-start.3) | async-done | bytes 1081376 | tf_op jit(solution)/shard_map/all_to_all | solution.py:58
  97.3 0.7 copy.15
  (24 shorter events, 0.8 us)
Async XLA Ops:
  12.6 31.5 %all-to-all-start.1 = ((bf16[8,16,1024]{2,1,0:T(8,128)(2,1)}), bf16[8,16,1024]{2,1,0:T(8,128)(2,1)S(1)}, u32[]{:S(2)}, u32[]{:S(2)}) async-start(bf16[8,16,1024]{2,1,0:T(8,128)(2,1)} %pad_maximum_fusion.4), calls=%async_computation.1 | async-start | bytes 524288 | tf_op jit(solution)/shard_map/all_to_all | solution.py:35
  26.6 28.6 %collective-permute-start = (bf16[4,1,16,1024]{3,2,0,1:T(8,128)(2,1)S(1)}, bf16[4,1,16,1024]{3,2,0,1:T(8,128)(2,1)S(1)}, u32[]{:S(2)}, u32[]{:S(2)}) collective-permute-start(bf16[4,1,16,1024]{3,2,0,1:T(8,128)(2,1)S(1)} %bitcast.75), channel_id=1, source_target_pairs={{0,8},{4,12},{8,0},{12,4},{1,9},{5,13},{9,1},{13,5},{2,10},{6,14},... | collective-permute-start | bytes 393224 | tf_op jit(solution)/shard_map/ppermute | solution.py:45
  45.3 26.0 %all-to-all-start.2 = ((bf16[4,128,1024]{2,1,0:T(8,128)(2,1)}), bf16[4,128,1024]{2,1,0:T(8,128)(2,1)S(1)}, u32[]{:S(2)}, u32[]{:S(2)}) async-start(bf16[4,128,1024]{2,1,0:T(8,128)(2,1)} %broadcast_in_dim.7), calls=%async_computation.2 | async-start | bytes 2097152 | tf_op jit(solution)/shard_map/all_to_all | solution.py:37
  55.2 10.3 %collective-permute-start.1 = (bf16[4,2,16,1024]{3,2,1,0:T(8,128)(2,1)S(1)}, bf16[4,2,16,1024]{3,2,1,0:T(8,128)(2,1)S(1)}, u32[]{:S(2)}, u32[]{:S(2)}) collective-permute-start(bf16[4,2,16,1024]{3,2,1,0:T(8,128)(2,1)S(1)} %get-tuple-element.30), channel_id=1, source_target_pairs={{0,4},{4,0},{8,12},{12,8},{1,5},{5,1},{9,13},{13,9},{2,6},{6,2},{1... | collective-permute-start | bytes 786440 | tf_op jit(solution)/shard_map/ppermute | solution.py:45
  65.5 7.7 %collective-permute-start.2 = (bf16[4,4,16,1024]{3,2,1,0:T(8,128)(2,1)S(1)}, bf16[4,4,16,1024]{3,2,1,0:T(8,128)(2,1)S(1)}, u32[]{:S(2)}, u32[]{:S(2)}) collective-permute-start(bf16[4,4,16,1024]{3,2,1,0:T(8,128)(2,1)S(1)} %bitcast.68), channel_id=1, source_target_pairs={{0,1},{1,0},{2,3},{3,2},{4,5},{5,4},{6,7},{7,6},{8,9},{9,8},{10,11... | collective-permute-start | bytes 1572872 | tf_op jit(solution)/shard_map/ppermute | solution.py:47
  71.3 3.8 %collective-permute-start.3 = (bf16[2,128,1024]{2,1,0:T(8,128)(2,1)S(1)}, bf16[2,128,1024]{2,1,0:T(8,128)(2,1)S(1)}, u32[]{:S(2)}, u32[]{:S(2)}) collective-permute-start(bf16[2,128,1024]{2,1,0:T(8,128)(2,1)S(1)} %dynamic-slice_bitcast_fusion), channel_id=1, source_target_pairs={{0,1},{1,0},{2,3},{3,2},{4,5},{5,4},{6,7},{7,6},{8,9},{9,8},{10,11... | collective-permute-start | bytes 1572872 | tf_op jit(solution)/shard_map/ppermute | solution.py:40
  77.2 19.6 %all-to-all-start.3 = ((f32[8,264,128]{2,1,0:T(8,128)}), f32[8,264,128]{2,1,0:T(8,128)S(1)}, u32[]{:S(2)}, u32[]{:S(2)}) async-start(f32[8,264,128]{2,1,0:T(8,128)} %bitcast.31), calls=%async_computation.3 | async-start | bytes 2162688 | tf_op jit(solution)/shard_map/all_to_all | solution.py:58

commit v8 on v7

--- a/solution.py
+++ b/solution.py
@@ -36,14 +36,14 @@
     columns = columns.reshape(16 * count, part)
     columns = lax.all_to_all(jnp.broadcast_to(columns[None], (4, *columns.shape)), ("xh", "xl"), 0, 0)
     columns = columns.reshape(2, 2, 16 * count, part)
-    own = lax.dynamic_index_in_dim(columns, core, 1, keepdims=False)
-    other = lax.ppermute(lax.dynamic_index_in_dim(columns, 1 - core, 1, keepdims=False), "core", TRADE)
-    blocks = [block.reshape(32 * count, part) for block in (own, other)]
-
     rows = held[:, None]
     for step in (2, 1):
         other = lax.ppermute(rows, "za", [(z, z ^ step) for z in range(4)])
         rows = jnp.stack([rows, other], axis=2).reshape(4, -1, 2 * count, part)
+    columns, rows = lax.optimization_barrier((columns, rows))
+    own = lax.dynamic_index_in_dim(columns, core, 1, keepdims=False)
+    other = lax.ppermute(lax.dynamic_index_in_dim(columns, 1 - core, 1, keepdims=False), "core", TRADE)
+    blocks = [block.reshape(32 * count, part) for block in (own, other)]
     other = lax.ppermute(rows, "core", TRADE)
     rows = jnp.stack([rows, other], axis=1).reshape(4, 16 * count, part)
 

time: 98.4 us -> 109 us (1.11)
  blocking collectives: 11.9 us -> 43.2 us
  starting transfers between devices: 38.3 us -> 18.1 us
    all_to_all x0 -> x1, blocking collectives: none -> 31.3 us  [body(): columns = lax.all_to_all(jnp.concatenate([held, held]), ('zh', 'za'), 0, 0)]
    all_to_all x1 -> x0, starting transfers between devices: 13.9 us -> none  [body(): columns = lax.all_to_all(jnp.concatenate([held, held]), ('zh', 'za'), 0, 0)]
    all_to_all x1 -> x0, waiting for transfers between devices: 10.3 us -> none  [body(): columns = lax.all_to_all(jnp.concatenate([held, held]), ('zh', 'za'), 0, 0)]
    ppermute x2, waiting for transfers between devices: 14.2 us -> 24 us  [body(): other = lax.ppermute(rows, 'za', [(z, z ^ step) for z in range(4)])]
    ppermute x2, starting transfers between devices: 9.19 us -> 3.83 us  [body(): other = lax.ppermute(rows, 'za', [(z, z ^ step) for z in range(4)])]
  transfers between devices with their start and end apart: 7 -> 6, of which waited for: 5 -> 4; matrix products, arithmetic and copies ran while one was open for 2% -> 1% of each run, Pallas kernels for 0% -> 0%
where the time goes in v8:
time: 109 us; the launch traced here: 108 us
  blocking collectives  43.2 us (40%)
  waiting for transfers between devices  40.8 us (37%)
  starting transfers between devices  18.1 us (17%)
  local copies, waits for them, and re-layouts  3.31 us (3%)
  other arithmetic  1.23 us (1%)
    all_to_all x1, blocking collectives, body(): columns = lax.all_to_all(jnp.concatenate([held, held]), ('zh', 'za'), 0, 0)  31.3 us
    ppermute x2, waiting for transfers between devices, body(): other = lax.ppermute(rows, 'za', [(z, z ^ step) for z in range(4)])  24 us
    all_to_all x1, waiting for transfers between devices, body(): lax.all_to_all(message.reshape(8, -1, 16 * count), SUM, 0, 0)  16 us
    all_to_all x1, blocking collectives, body(): lax.all_to_all(grads.reshape(count, 8, part).transpose(1, 0, 2), SUM, 0, 0)  11.9 us
    ppermute x1, starting transfers between devices, body(): other = lax.ppermute(rows, 'core', TRADE)  4.76 us
    all_to_all x1, starting transfers between devices, body(): lax.all_to_all(jnp.broadcast_to(columns[None], (4, *columns.shape)), ('xh...  4.01 us
    ppermute x2, starting transfers between devices, body(): other = lax.ppermute(rows, 'za', [(z, z ^ step) for z in range(4)])  3.83 us
    all_to_all x1, starting transfers between devices, body(): lax.all_to_all(message.reshape(8, -1, 16 * count), SUM, 0, 0)  3.56 us
  transfers between devices with their start and end apart: 6, of which 4 were waited for; matrix products, arithmetic and copies ran while one was open for 1% of the time, Pallas kernels for 0%

profile of v8, /device:TPU:1, one launch (start us, length us, event | category | flops | bytes accessed | tf_op | source)
XLA Modules:
  0.0 107.8 jit_solution(295822748592338195)
XLA Ops:
  0.0 11.9 %all_to_all.20 = bf16[8,8,1024]{2,1,0:T(8,128)(2,1)S(1)} all-to-all(bf16[8,8,1024]{2,1,0:T(8,128)(2,1)} %bitcast.84), channel_id=1, replica_groups=mesh['y'=4,'xh'=2,'xl'=2,'zh'=2,'za'=4,'zb'=2,'core'=2] {'y','zb'}, dimensions={0} | all-to-all | bytes 262144 | tf_op jit(solution)/shard_map/all_to_all | solution.py:32
  11.9 31.3 %all_to_all.21 = bf16[8,16,1024]{2,1,0:T(8,128)(2,1)S(1)} all-to-all(bf16[8,16,1024]{2,1,0:T(8,128)(2,1)S(1)} %pad_maximum_fusion.4), channel_id=1, replica_groups=mesh['y'=4,'xh'=2,'xl'=2,'zh'=2,'za'=4,'zb'=2,'core'=2] {'zh','za'}, dimensions={0} | all-to-all | bytes 524288 | tf_op jit(solution)/shard_map/all_to_all | solution.py:35
  43.2 1.1 %broadcast_in_dim.7 = bf16[4,128,1024]{2,1,0:T(8,128)(2,1)} broadcast(bf16[128,1024]{1,0:T(8,128)(2,1)S(1)} %bitcast.79), dimensions={1,2} | broadcast | bytes 1310720 | tf_op jit(solution)/shard_map/broadcast_in_dim | solution.py:37
  44.4 4.0 %all-to-all-start.2 = ((bf16[4,128,1024]{2,1,0:T(8,128)(2,1)}), bf16[4,128,1024]{2,1,0:T(8,128)(2,1)S(1)}, u32[]{:S(2)}, u32[]{:S(2)}) async-start(bf16[4,128,1024]{2,1,0:T(8,128)(2,1)} %broadcast_in_dim.7), calls=%async_computation.2 | async-start | bytes 2097152 | tf_op jit(solution)/shard_map/all_to_all | solution.py:37
  48.4 1.9 %collective-permute-start = (bf16[4,1,16,1024]{3,2,0,1:T(8,128)(2,1)S(1)}, bf16[4,1,16,1024]{3,2,0,1:T(8,128)(2,1)S(1)}, u32[]{:S(2)}, u32[]{:S(2)}) collective-permute-start(bf16[4,1,16,1024]{3,2,0,1:T(8,128)(2,1)S(1)} %bitcast.77), channel_id=1, source_target_pairs={{0,8},{4,12},{8,0},{12,4},{1,9},{5,13},{9,1},{13,5},{2,10},{6,14},... | collective-permute-start | bytes 393224 | tf_op jit(solution)/shard_map/ppermute | solution.py:41
  50.3 11.2 %collective-permute-done = bf16[4,1,16,1024]{3,2,0,1:T(8,128)(2,1)S(1)} collective-permute-done((bf16[4,1,16,1024]{3,2,0,1:T(8,128)(2,1)S(1)}, bf16[4,1,16,1024]{3,2,0,1:T(8,128)(2,1)S(1)}, u32[]{:S(2)}, u32[]{:S(2)}) %collective-permute-start) | collective-permute-done | bytes 131104 | tf_op jit(solution)/shard_map/ppermute | solution.py:41
  61.5 1.9 %collective-permute-start.1 = (bf16[4,2,16,1024]{3,2,1,0:T(8,128)(2,1)S(1)}, bf16[4,2,16,1024]{3,2,1,0:T(8,128)(2,1)S(1)}, u32[]{:S(2)}, u32[]{:S(2)}) collective-permute-start(bf16[4,2,16,1024]{3,2,1,0:T(8,128)(2,1)S(1)} %get-tuple-element.34), channel_id=1, source_target_pairs={{0,4},{4,0},{8,12},{12,8},{1,5},{5,1},{9,13},{13,9},{2,6},{6,2},{1... | collective-permute-start | bytes 786440 | tf_op jit(solution)/shard_map/ppermute | solution.py:41
  63.4 12.8 %collective-permute-done.1 = bf16[4,2,16,1024]{3,2,1,0:T(8,128)(2,1)S(1)} collective-permute-done((bf16[4,2,16,1024]{3,2,1,0:T(8,128)(2,1)S(1)}, bf16[4,2,16,1024]{3,2,1,0:T(8,128)(2,1)S(1)}, u32[]{:S(2)}, u32[]{:S(2)}) %collective-permute-start.1) | collective-permute-done | bytes 262176 | tf_op jit(solution)/shard_map/ppermute | solution.py:41
  76.3 4.8 %collective-permute-start.2 = (bf16[4,4,16,1024]{3,2,1,0:T(8,128)(2,1)S(1)}, bf16[4,4,16,1024]{3,2,1,0:T(8,128)(2,1)S(1)}, u32[]{:S(2)}, u32[]{:S(2)}) collective-permute-start(bf16[4,4,16,1024]{3,2,1,0:T(8,128)(2,1)S(1)} %bitcast.70), channel_id=1, source_target_pairs={{0,1},{1,0},{2,3},{3,2},{4,5},{5,4},{6,7},{7,6},{8,9},{9,8},{10,11... | collective-permute-start | bytes 1572872 | tf_op jit(solution)/shard_map/ppermute | solution.py:47
  81.2 1.9 %collective-permute-start.3 = (bf16[2,128,1024]{2,1,0:T(8,128)(2,1)S(1)}, bf16[2,128,1024]{2,1,0:T(8,128)(2,1)S(1)}, u32[]{:S(2)}, u32[]{:S(2)}) collective-permute-start(bf16[2,128,1024]{2,1,0:T(8,128)(2,1)S(1)} %dynamic-slice_bitcast_fusion), channel_id=1, source_target_pairs={{0,1},{1,0},{2,3},{3,2},{4,5},{5,4},{6,7},{7,6},{8,9},{9,8},{10,11... | collective-permute-start | bytes 1572872 | tf_op jit(solution)/shard_map/ppermute | solution.py:45
  83.1 0.2 multiply_reduce_fusion.2
  83.3 0.3 multiply_reduce_fusion
  83.7 0.1 pad_maximum_fusion.1
  83.8 0.5 convolution_bitcast_fusion.1
  84.3 0.7 collective-permute-done.3
  85.0 0.5 convolution_bitcast_fusion
  85.6 0.2 multiply_reduce_fusion.1
  85.8 0.1 scatter.9
  86.1 1.1 copy.15
  87.1 3.6 %all-to-all-start.3 = ((f32[8,264,128]{2,1,0:T(8,128)}), f32[8,264,128]{2,1,0:T(8,128)S(1)}, u32[]{:S(2)}, u32[]{:S(2)}) async-start(f32[8,264,128]{2,1,0:T(8,128)} %bitcast.32), calls=%async_computation.3 | async-start | bytes 2162688 | tf_op jit(solution)/shard_map/all_to_all | solution.py:58
  90.7 16.0 %all-to-all-done.3 = f32[8,264,128]{2,1,0:T(8,128)S(1)} async-done(((f32[8,264,128]{2,1,0:T(8,128)}), f32[8,264,128]{2,1,0:T(8,128)S(1)}, u32[]{:S(2)}, u32[]{:S(2)}) %all-to-all-start.3) | async-done | bytes 1081376 | tf_op jit(solution)/shard_map/all_to_all | solution.py:58
  106.8 0.1 fusion.7
  107.0 0.1 copy.17
  107.1 0.7 copy.18
  (23 shorter events, 0.6 us)
Async XLA Ops:
  44.4 32.0 %all-to-all-start.2 = ((bf16[4,128,1024]{2,1,0:T(8,128)(2,1)}), bf16[4,128,1024]{2,1,0:T(8,128)(2,1)S(1)}, u32[]{:S(2)}, u32[]{:S(2)}) async-start(bf16[4,128,1024]{2,1,0:T(8,128)(2,1)} %broadcast_in_dim.7), calls=%async_computation.2 | async-start | bytes 2097152 | tf_op jit(solution)/shard_map/all_to_all | solution.py:37
  48.4 13.1 %collective-permute-start = (bf16[4,1,16,1024]{3,2,0,1:T(8,128)(2,1)S(1)}, bf16[4,1,16,1024]{3,2,0,1:T(8,128)(2,1)S(1)}, u32[]{:S(2)}, u32[]{:S(2)}) collective-permute-start(bf16[4,1,16,1024]{3,2,0,1:T(8,128)(2,1)S(1)} %bitcast.77), channel_id=1, source_target_pairs={{0,8},{4,12},{8,0},{12,4},{1,9},{5,13},{9,1},{13,5},{2,10},{6,14},... | collective-permute-start | bytes 393224 | tf_op jit(solution)/shard_map/ppermute | solution.py:41
  61.5 14.8 %collective-permute-start.1 = (bf16[4,2,16,1024]{3,2,1,0:T(8,128)(2,1)S(1)}, bf16[4,2,16,1024]{3,2,1,0:T(8,128)(2,1)S(1)}, u32[]{:S(2)}, u32[]{:S(2)}) collective-permute-start(bf16[4,2,16,1024]{3,2,1,0:T(8,128)(2,1)S(1)} %get-tuple-element.34), channel_id=1, source_target_pairs={{0,4},{4,0},{8,12},{12,8},{1,5},{5,1},{9,13},{13,9},{2,6},{6,2},{1... | collective-permute-start | bytes 786440 | tf_op jit(solution)/shard_map/ppermute | solution.py:41
  76.3 6.9 %collective-permute-start.2 = (bf16[4,4,16,1024]{3,2,1,0:T(8,128)(2,1)S(1)}, bf16[4,4,16,1024]{3,2,1,0:T(8,128)(2,1)S(1)}, u32[]{:S(2)}, u32[]{:S(2)}) collective-permute-start(bf16[4,4,16,1024]{3,2,1,0:T(8,128)(2,1)S(1)} %bitcast.70), channel_id=1, source_target_pairs={{0,1},{1,0},{2,3},{3,2},{4,5},{5,4},{6,7},{7,6},{8,9},{9,8},{10,11... | collective-permute-start | bytes 1572872 | tf_op jit(solution)/shard_map/ppermute | solution.py:47
  81.2 3.8 %collective-permute-start.3 = (bf16[2,128,1024]{2,1,0:T(8,128)(2,1)S(1)}, bf16[2,128,1024]{2,1,0:T(8,128)(2,1)S(1)}, u32[]{:S(2)}, u32[]{:S(2)}) collective-permute-start(bf16[2,128,1024]{2,1,0:T(8,128)(2,1)S(1)} %dynamic-slice_bitcast_fusion), channel_id=1, source_target_pairs={{0,1},{1,0},{2,3},{3,2},{4,5},{5,4},{6,7},{7,6},{8,9},{9,8},{10,11... | collective-permute-start | bytes 1572872 | tf_op jit(solution)/shard_map/ppermute | solution.py:45
  87.1 19.6 %all-to-all-start.3 = ((f32[8,264,128]{2,1,0:T(8,128)}), f32[8,264,128]{2,1,0:T(8,128)S(1)}, u32[]{:S(2)}, u32[]{:S(2)}) async-start(f32[8,264,128]{2,1,0:T(8,128)} %bitcast.32), calls=%async_computation.3 | async-start | bytes 2162688 | tf_op jit(solution)/shard_map/all_to_all | solution.py:58

commit v9 on v7

--- a/solution.py
+++ b/solution.py
@@ -49,13 +49,13 @@
 
     lines = rows.reshape(64 * count, part)
     products = jnp.stack([cross(block, lines).reshape(2, 16 * count, 4, -1) for block in blocks], axis=1)
-    products = products.reshape(2, 32 * count, 4, -1).transpose(2, 0, 1, 3)
+    products = products.reshape(2, 32 * count, 4, -1).swapaxes(1, 2)
     wide = jnp.stack([squares(block).reshape(2, -1) for block in blocks], axis=1)
-    extra = jnp.zeros((4, 2, 8, 16 * count), jnp.float32)
-    extra = extra.at[:, :, 0].set(squares(rows)[:, None])
-    extra = extra.at[:, :, 1:3].set(wide[None])
+    extra = jnp.zeros((2, 4, 8, 16 * count), jnp.float32)
+    extra = extra.at[:, :, 0].set(squares(rows)[None])
+    extra = extra.at[:, :, 1:3].set(wide[:, None])
     message = jnp.concatenate([products, extra], axis=2)
-    total = jnp.sum(lax.all_to_all(message.reshape(8, -1, 16 * count), SUM, 0, 0), axis=0)
+    total = jnp.sum(lax.all_to_all(message.reshape(8, -1, 16 * count), ("zb", "y"), 0, 0), axis=0)
     gram, extra = total[: 32 * count], lax.rsqrt(total[32 * count :] + 1e-06)
     gram = gram * extra[1:3].reshape(-1)[:, None] * extra[0]
 

time: 98.4 us -> 97.6 us (level)
  local copies, waits for them, and re-layouts: 3.32 us -> 2.25 us
  other arithmetic: 1.93 us -> 2.92 us
    concatenate x1 -> x0, local copies, waits for them, and re-layouts: 1.06 us -> none  [body(): message = jnp.concatenate([products, extra], axis=2)]
    concatenate x1, other arithmetic: 0.07 us -> 1.06 us  [body(): message = jnp.concatenate([products, extra], axis=2)]
where the time goes in v9:
time: 97.6 us; the launch traced here: 97.1 us
  waiting for transfers between devices  40.5 us (41%)
  starting transfers between devices  38.3 us (39%)
  blocking collectives  11.9 us (12%)
  other arithmetic  2.92 us (3%)
  local copies, waits for them, and re-layouts  2.25 us (2%)
    all_to_all x1, waiting for transfers between devices, body(): lax.all_to_all(message.reshape(8, -1, 16 * count), ('zb', 'y'), 0, 0)  15.3 us
    ppermute x2, waiting for transfers between devices, body(): other = lax.ppermute(rows, 'za', [(z, z ^ step) for z in range(4)])  14.2 us
    all_to_all x1, starting transfers between devices, body(): columns = lax.all_to_all(jnp.concatenate([held, held]), ('zh', 'za'), 0, 0)  13.9 us
    all_to_all x1, blocking collectives, body(): lax.all_to_all(grads.reshape(count, 8, part).transpose(1, 0, 2), SUM, 0, 0)  11.9 us
    all_to_all x1, waiting for transfers between devices, body(): columns = lax.all_to_all(jnp.concatenate([held, held]), ('zh', 'za'), 0, 0)  10.3 us
    ppermute x2, starting transfers between devices, body(): other = lax.ppermute(rows, 'za', [(z, z ^ step) for z in range(4)])  9.19 us
    ppermute x1, starting transfers between devices, body(): other = lax.ppermute(rows, 'core', TRADE)  5.72 us
    all_to_all x1, starting transfers between devices, body(): lax.all_to_all(jnp.broadcast_to(columns[None], (4, *columns.shape)), ('xh...  4.01 us
  transfers between devices with their start and end apart: 7, of which 5 were waited for; matrix products, arithmetic and copies ran while one was open for 2% of the time, Pallas kernels for 0%

profile of v9, /device:TPU:1, one launch (start us, length us, event | category | flops | bytes accessed | tf_op | source)
XLA Modules:
  0.0 97.1 jit_solution(14536799259780886276)
XLA Ops:
  0.0 11.9 %all_to_all.20 = bf16[8,8,1024]{2,1,0:T(8,128)(2,1)S(1)} all-to-all(bf16[8,8,1024]{2,1,0:T(8,128)(2,1)} %bitcast.82), channel_id=1, replica_groups=mesh['y'=4,'xh'=2,'xl'=2,'zh'=2,'za'=4,'zb'=2,'core'=2] {'y','zb'}, dimensions={0} | all-to-all | bytes 262144 | tf_op jit(solution)/shard_map/all_to_all | solution.py:32
  11.9 0.7 pad_maximum_fusion.4
  12.6 13.9 %all-to-all-start.1 = ((bf16[8,16,1024]{2,1,0:T(8,128)(2,1)}), bf16[8,16,1024]{2,1,0:T(8,128)(2,1)S(1)}, u32[]{:S(2)}, u32[]{:S(2)}) async-start(bf16[8,16,1024]{2,1,0:T(8,128)(2,1)} %pad_maximum_fusion.4), calls=%async_computation.1 | async-start | bytes 524288 | tf_op jit(solution)/shard_map/all_to_all | solution.py:35
  26.6 7.3 %collective-permute-start = (bf16[4,1,16,1024]{3,2,0,1:T(8,128)(2,1)S(1)}, bf16[4,1,16,1024]{3,2,0,1:T(8,128)(2,1)S(1)}, u32[]{:S(2)}, u32[]{:S(2)}) collective-permute-start(bf16[4,1,16,1024]{3,2,0,1:T(8,128)(2,1)S(1)} %bitcast.75), channel_id=1, source_target_pairs={{0,8},{4,12},{8,0},{12,4},{1,9},{5,13},{9,1},{13,5},{2,10},{6,14},... | collective-permute-start | bytes 393224 | tf_op jit(solution)/shard_map/ppermute | solution.py:45
  33.8 10.3 %all-to-all-done.1 = bf16[8,16,1024]{2,1,0:T(8,128)(2,1)S(1)} async-done(((bf16[8,16,1024]{2,1,0:T(8,128)(2,1)}), bf16[8,16,1024]{2,1,0:T(8,128)(2,1)S(1)}, u32[]{:S(2)}, u32[]{:S(2)}) %all-to-all-start.1) | async-done | bytes 262176 | tf_op jit(solution)/shard_map/all_to_all | solution.py:35
  44.1 1.1 %broadcast_in_dim.7 = bf16[4,128,1024]{2,1,0:T(8,128)(2,1)} broadcast(bf16[128,1024]{1,0:T(8,128)(2,1)S(1)} %bitcast.77), dimensions={1,2} | broadcast | bytes 1310720 | tf_op jit(solution)/shard_map/broadcast_in_dim | solution.py:37
  45.3 4.0 %all-to-all-start.2 = ((bf16[4,128,1024]{2,1,0:T(8,128)(2,1)}), bf16[4,128,1024]{2,1,0:T(8,128)(2,1)S(1)}, u32[]{:S(2)}, u32[]{:S(2)}) async-start(bf16[4,128,1024]{2,1,0:T(8,128)(2,1)} %broadcast_in_dim.7), calls=%async_computation.2 | async-start | bytes 2097152 | tf_op jit(solution)/shard_map/all_to_all | solution.py:37
  49.3 5.9 %collective-permute-done = bf16[4,1,16,1024]{3,2,0,1:T(8,128)(2,1)S(1)} collective-permute-done((bf16[4,1,16,1024]{3,2,0,1:T(8,128)(2,1)S(1)}, bf16[4,1,16,1024]{3,2,0,1:T(8,128)(2,1)S(1)}, u32[]{:S(2)}, u32[]{:S(2)}) %collective-permute-start) | collective-permute-done | bytes 131104 | tf_op jit(solution)/shard_map/ppermute | solution.py:45
  55.2 1.9 %collective-permute-start.1 = (bf16[4,2,16,1024]{3,2,1,0:T(8,128)(2,1)S(1)}, bf16[4,2,16,1024]{3,2,1,0:T(8,128)(2,1)S(1)}, u32[]{:S(2)}, u32[]{:S(2)}) collective-permute-start(bf16[4,2,16,1024]{3,2,1,0:T(8,128)(2,1)S(1)} %get-tuple-element.30), channel_id=1, source_target_pairs={{0,4},{4,0},{8,12},{12,8},{1,5},{5,1},{9,13},{13,9},{2,6},{6,2},{1... | collective-permute-start | bytes 786440 | tf_op jit(solution)/shard_map/ppermute | solution.py:45
  57.1 8.3 %collective-permute-done.1 = bf16[4,2,16,1024]{3,2,1,0:T(8,128)(2,1)S(1)} collective-permute-done((bf16[4,2,16,1024]{3,2,1,0:T(8,128)(2,1)S(1)}, bf16[4,2,16,1024]{3,2,1,0:T(8,128)(2,1)S(1)}, u32[]{:S(2)}, u32[]{:S(2)}) %collective-permute-start.1) | collective-permute-done | bytes 262176 | tf_op jit(solution)/shard_map/ppermute | solution.py:45
  65.5 5.7 %collective-permute-start.2 = (bf16[4,4,16,1024]{3,2,1,0:T(8,128)(2,1)S(1)}, bf16[4,4,16,1024]{3,2,1,0:T(8,128)(2,1)S(1)}, u32[]{:S(2)}, u32[]{:S(2)}) collective-permute-start(bf16[4,4,16,1024]{3,2,1,0:T(8,128)(2,1)S(1)} %bitcast.68), channel_id=1, source_target_pairs={{0,1},{1,0},{2,3},{3,2},{4,5},{5,4},{6,7},{7,6},{8,9},{9,8},{10,11... | collective-permute-start | bytes 1572872 | tf_op jit(solution)/shard_map/ppermute | solution.py:47
  71.3 1.9 %collective-permute-start.3 = (bf16[2,128,1024]{2,1,0:T(8,128)(2,1)S(1)}, bf16[2,128,1024]{2,1,0:T(8,128)(2,1)S(1)}, u32[]{:S(2)}, u32[]{:S(2)}) collective-permute-start(bf16[2,128,1024]{2,1,0:T(8,128)(2,1)S(1)} %dynamic-slice_bitcast_fusion), channel_id=1, source_target_pairs={{0,1},{1,0},{2,3},{3,2},{4,5},{5,4},{6,7},{7,6},{8,9},{9,8},{10,11... | collective-permute-start | bytes 1572872 | tf_op jit(solution)/shard_map/ppermute | solution.py:40
  73.2 0.3 multiply_reduce_fusion
  73.6 0.1 pad_maximum_fusion.1
  73.7 0.2 multiply_reduce_fusion.2
  73.9 0.5 convolution_bitcast_fusion.1
  74.4 0.7 collective-permute-done.3
  75.1 0.5 convolution_bitcast_fusion
  75.7 0.2 multiply_reduce_fusion.1
  76.0 0.1 scatter.9
  76.1 1.1 %pad_maximum_fusion = f32[2,4,264,128]{3,2,1,0:T(8,128)} fusion(f32[2,4,8,128]{3,2,1,0:T(8,128)S(1)} %scatter.9, f32[2,4,256,128]{3,2,1,0:T(8,128)S(1)} %bitcast.71), kind=kLoop, calls=%fused_computation.3 | loop fusion | flops 270336 | bytes 2162688 | tf_op jit(solution)/shard_map/concatenate | solution.py:57
  77.2 3.6 %all-to-all-start.3 = ((f32[8,264,128]{2,1,0:T(8,128)}), f32[8,264,128]{2,1,0:T(8,128)S(1)}, u32[]{:S(2)}, u32[]{:S(2)}) async-start(f32[8,264,128]{2,1,0:T(8,128)} %bitcast.31), calls=%async_computation.3 | async-start | bytes 2162688 | tf_op jit(solution)/shard_map/all_to_all | solution.py:58
  80.7 15.3 %all-to-all-done.3 = f32[8,264,128]{2,1,0:T(8,128)S(1)} async-done(((f32[8,264,128]{2,1,0:T(8,128)}), f32[8,264,128]{2,1,0:T(8,128)S(1)}, u32[]{:S(2)}, u32[]{:S(2)}) %all-to-all-start.3) | async-done | bytes 1081376 | tf_op jit(solution)/shard_map/all_to_all | solution.py:58
  96.4 0.7 copy.13
  (23 shorter events, 0.7 us)
Async XLA Ops:
  12.6 31.5 %all-to-all-start.1 = ((bf16[8,16,1024]{2,1,0:T(8,128)(2,1)}), bf16[8,16,1024]{2,1,0:T(8,128)(2,1)S(1)}, u32[]{:S(2)}, u32[]{:S(2)}) async-start(bf16[8,16,1024]{2,1,0:T(8,128)(2,1)} %pad_maximum_fusion.4), calls=%async_computation.1 | async-start | bytes 524288 | tf_op jit(solution)/shard_map/all_to_all | solution.py:35
  26.6 28.6 %collective-permute-start = (bf16[4,1,16,1024]{3,2,0,1:T(8,128)(2,1)S(1)}, bf16[4,1,16,1024]{3,2,0,1:T(8,128)(2,1)S(1)}, u32[]{:S(2)}, u32[]{:S(2)}) collective-permute-start(bf16[4,1,16,1024]{3,2,0,1:T(8,128)(2,1)S(1)} %bitcast.75), channel_id=1, source_target_pairs={{0,8},{4,12},{8,0},{12,4},{1,9},{5,13},{9,1},{13,5},{2,10},{6,14},... | collective-permute-start | bytes 393224 | tf_op jit(solution)/shard_map/ppermute | solution.py:45
  45.3 26.0 %all-to-all-start.2 = ((bf16[4,128,1024]{2,1,0:T(8,128)(2,1)}), bf16[4,128,1024]{2,1,0:T(8,128)(2,1)S(1)}, u32[]{:S(2)}, u32[]{:S(2)}) async-start(bf16[4,128,1024]{2,1,0:T(8,128)(2,1)} %broadcast_in_dim.7), calls=%async_computation.2 | async-start | bytes 2097152 | tf_op jit(solution)/shard_map/all_to_all | solution.py:37
  55.2 10.3 %collective-permute-start.1 = (bf16[4,2,16,1024]{3,2,1,0:T(8,128)(2,1)S(1)}, bf16[4,2,16,1024]{3,2,1,0:T(8,128)(2,1)S(1)}, u32[]{:S(2)}, u32[]{:S(2)}) collective-permute-start(bf16[4,2,16,1024]{3,2,1,0:T(8,128)(2,1)S(1)} %get-tuple-element.30), channel_id=1, source_target_pairs={{0,4},{4,0},{8,12},{12,8},{1,5},{5,1},{9,13},{13,9},{2,6},{6,2},{1... | collective-permute-start | bytes 786440 | tf_op jit(solution)/shard_map/ppermute | solution.py:45
  65.5 7.7 %collective-permute-start.2 = (bf16[4,4,16,1024]{3,2,1,0:T(8,128)(2,1)S(1)}, bf16[4,4,16,1024]{3,2,1,0:T(8,128)(2,1)S(1)}, u32[]{:S(2)}, u32[]{:S(2)}) collective-permute-start(bf16[4,4,16,1024]{3,2,1,0:T(8,128)(2,1)S(1)} %bitcast.68), channel_id=1, source_target_pairs={{0,1},{1,0},{2,3},{3,2},{4,5},{5,4},{6,7},{7,6},{8,9},{9,8},{10,11... | collective-permute-start | bytes 1572872 | tf_op jit(solution)/shard_map/ppermute | solution.py:47
  71.3 3.8 %collective-permute-start.3 = (bf16[2,128,1024]{2,1,0:T(8,128)(2,1)S(1)}, bf16[2,128,1024]{2,1,0:T(8,128)(2,1)S(1)}, u32[]{:S(2)}, u32[]{:S(2)}) collective-permute-start(bf16[2,128,1024]{2,1,0:T(8,128)(2,1)S(1)} %dynamic-slice_bitcast_fusion), channel_id=1, source_target_pairs={{0,1},{1,0},{2,3},{3,2},{4,5},{5,4},{6,7},{7,6},{8,9},{9,8},{10,11... | collective-permute-start | bytes 1572872 | tf_op jit(solution)/shard_map/ppermute | solution.py:40
  77.2 18.9 %all-to-all-start.3 = ((f32[8,264,128]{2,1,0:T(8,128)}), f32[8,264,128]{2,1,0:T(8,128)S(1)}, u32[]{:S(2)}, u32[]{:S(2)}) async-start(f32[8,264,128]{2,1,0:T(8,128)} %bitcast.31), calls=%async_computation.3 | async-start | bytes 2162688 | tf_op jit(solution)/shard_map/all_to_all | solution.py:58
